TPU v7x, 128 devices: a whole 4x4x4 slice. The times are simulated.
128 devices in a mesh: row: 8 (over z, core), col: 16 (over x, y).
Axes of the slice: x: 4, y: 4, z: 4, core: 2. Of those that a mesh axis runs over, the one named last changes fastest.
Arguments:
- pair: bfloat16 [2048, 2048, 128], P('row', 'col'), may hold values from -6 to 6
- node_state: bfloat16 [2048, 64], P(('row', 'col')), may hold values from -6 to 6
- coords: float32 [3, 3, 2048], P(None, None, ('row', 'col')), may hold values from -8 to 8
- neighbours: int32 [2048, 64], P('row'), may hold values from 0 to 2047, as said below
- chain: int32 [2048], replicated, may hold values from 0 to 3, never falling along the last dimension, each value on 1 to 1024 neighbouring positions
- w_edge: bfloat16 [128, 64], replicated, may hold values from -0.5 to 0.5
- w_radial: bfloat16 [36, 64], replicated, may hold values from -3 to 3
- w_query: bfloat16 [64, 64], replicated, may hold values from -0.75 to 0.75
- w_keyval: bfloat16 [64, 128], replicated, may hold values from -0.75 to 0.75
- w_edge_kv: bfloat16 [64, 128], replicated, may hold values from -0.75 to 0.75
- w_out: bfloat16 [64, 64], replicated, may hold values from -0.75 to 0.75
- w_move: bfloat16 [64, 12], replicated, may hold values from -0.75 to 0.75
- w_trans_in: bfloat16 [128, 256], replicated, may hold values from -0.5 to 0.5
- w_trans_out: bfloat16 [256, 128], replicated, may hold values from -0.375 to 0.375
- w_gate: bfloat16 [128, 128], replicated, may hold values from -0.5 to 0.5
- w_feat_in: bfloat16 [42, 128], replicated, may hold values from -3 to 3
- w_feat_out: bfloat16 [128, 128], replicated, may hold values from -0.5 to 0.5
Outputs:
- pair_out: bfloat16 [2048, 2048, 128], P('row', 'col')
- node_out: float32 [2048, 64], P(('row', 'col'))
- coords_out: float32 [3, 3, 2048], P(None, None, ('row', 'col'))
Inputs may be any that keep to these rules, and one draw needn't show every extreme that they name: Each row lists 64 distinct residues other than the residue itself. Among the neighbours of the 16 residues of one device (residues d * 16 to (d + 1) * 16 - 1), at most 128 lie in one column block of 128 residues, and exactly 128 lie in the column block that holds those residues.
All inputs are finite; a program needn't handle non-finite values.
Results may differ from a plain program's by a relative error of at most 0.0052.
Values may be sent and summed in bfloat16 or wider, within the bound.
No kernel may reach another device: no remote copies, remote signals or barrier semaphores. Data moves between devices by JAX's collectives and lax.ppermute only.
A program may use at most 128 MiB of HBM per device.

v0:
```python
import math

import jax
import jax.numpy as jnp
from jax import lax
from jax.sharding import PartitionSpec as P

HEADS = 4
K = 64
NRBF = 36


dist_top = 12.0
basis_width = 0.5


def radial_basis(distance):
    centres = jnp.arange(NRBF, dtype=jnp.float32) * (dist_top / (NRBF - 1))
    centres = centres.reshape((NRBF,) + (1,) * distance.ndim)
    return jnp.exp(-jnp.square((distance[None] - centres) / basis_width))


def edge_layer(
    edge_in,
    flat_lists,
    states,
    coords_own,
    keyval_all,
    coords_all,
    w_edge,
    w_radial,
    w_query,
    w_edge_kv,
    w_out,
    w_move,
):
    channels_node = states.shape[1]
    head_count = HEADS
    head_size = channels_node // head_count
    own_count = states.shape[0]
    edge_count = flat_lists.shape[0]
    nearby = coords_all[:, :, flat_lists]
    relative = nearby - jnp.repeat(coords_own, K, axis=2)
    distance = jnp.sqrt(jnp.sum(relative[1] * relative[1], axis=0))
    edge_basis = radial_basis(distance).astype(jnp.bfloat16)
    pre_act = jnp.dot(edge_in, w_edge, preferred_element_type=jnp.float32)
    pre_act = pre_act + lax.dot_general(
        edge_basis, w_radial, (((0,), (0,)), ((), ())), preferred_element_type=jnp.float32
    )
    edge_hidden = jax.nn.silu(pre_act).astype(jnp.bfloat16)
    edge_mix = jnp.dot(edge_hidden, w_edge_kv, preferred_element_type=jnp.float32)
    picked = keyval_all[flat_lists].astype(jnp.float32)
    key_part = picked[:, :channels_node] + edge_mix[:, :channels_node]
    values = picked[:, channels_node:] + edge_mix[:, channels_node:]
    queries = jnp.repeat(jnp.dot(states, w_query, preferred_element_type=jnp.float32), K, axis=0)
    logits = jnp.sum(
        (queries * key_part).reshape(edge_count, head_count, head_size), axis=2
    ) / math.sqrt(head_size)
    attention = jax.nn.sigmoid(logits)
    weighted = (attention[:, :, None] * values.reshape(edge_count, head_count, head_size)).reshape(
        own_count, K, channels_node
    )
    message = (jnp.sum(weighted, axis=1) / K).astype(jnp.bfloat16)
    node_out = states.astype(jnp.float32) + jnp.dot(
        message, w_out, preferred_element_type=jnp.float32
    )
    moves_raw = jnp.dot(edge_hidden, w_move, preferred_element_type=jnp.float32).reshape(
        edge_count, 3, head_count
    )
    move_coef = jnp.sum(moves_raw * attention[:, None, :], axis=2) / K
    coord_shift = jnp.sum(
        (jnp.transpose(move_coef)[:, None, :] * relative).reshape(3, 3, own_count, K), axis=3
    )
    return (node_out, coords_own + coord_shift)


def pair_features(row_x, col_x, row_chain, col_chain, row_pos, col_pos):
    alpha_row = row_x[1]
    alpha_col = col_x[1]
    displace = alpha_col[:, None, :] - alpha_row[:, :, None]
    distance = jnp.sqrt(jnp.sum(displace * displace, axis=0))
    inverse = 1.0 / (1.0 + distance)
    bond_rn = row_x[0] - alpha_row
    bond_rc = row_x[2] - alpha_row
    bond_cn = col_x[0] - alpha_col
    bond_cc = col_x[2] - alpha_col
    orient_rn = jnp.sum(bond_rn[:, :, None] * displace, axis=0) * inverse
    orient_rc = jnp.sum(bond_rc[:, :, None] * displace, axis=0) * inverse
    orient_cn = -jnp.sum(bond_cn[:, None, :] * displace, axis=0) * inverse
    orient_cc = -jnp.sum(bond_cc[:, None, :] * displace, axis=0) * inverse
    same_chain = (row_chain[:, None] == col_chain[None, :]).astype(jnp.float32)
    offset = (
        same_chain
        * jnp.clip(col_pos[None, :] - row_pos[:, None], -32, 32).astype(jnp.float32)
        / 32.0
    )
    tail_feats = jnp.stack([orient_rn, orient_rc, orient_cn, orient_cc, same_chain, offset], axis=0)
    return jnp.concatenate([radial_basis(distance), tail_feats], axis=0).astype(jnp.bfloat16)


def pair_update(pair_block, features, w_trans_in, w_trans_out, w_gate, w_feat_in, w_feat_out):
    row_count, col_width, channels = pair_block.shape
    flat_pair = pair_block.reshape(-1, channels).astype(jnp.float32)
    row_mean = jnp.mean(flat_pair, axis=1, keepdims=True)
    centred = flat_pair - row_mean
    normed = (
        centred * lax.rsqrt(jnp.mean(centred * centred, axis=1, keepdims=True) + 1e-05)
    ).astype(jnp.bfloat16)
    trans_hidden = jax.nn.relu(
        jnp.dot(normed, w_trans_in, preferred_element_type=jnp.float32)
    ).astype(jnp.bfloat16)
    trans_out = jnp.dot(trans_hidden, w_trans_out, preferred_element_type=jnp.float32)
    gate_val = jax.nn.sigmoid(jnp.dot(normed, w_gate, preferred_element_type=jnp.float32))
    feat_pre = lax.dot_general(
        features.reshape(features.shape[0], -1),
        w_feat_in,
        (((0,), (0,)), ((), ())),
        preferred_element_type=jnp.float32,
    )
    feat_hidden = jax.nn.silu(feat_pre).astype(jnp.bfloat16)
    struct_term = jnp.dot(feat_hidden, w_feat_out, preferred_element_type=jnp.float32)
    return (
        (flat_pair + trans_out + gate_val * struct_term)
        .astype(jnp.bfloat16)
        .reshape(row_count, col_width, channels)
    )


def local(
    pair,
    node_state,
    coords,
    neighbours,
    chain,
    w_edge,
    w_radial,
    w_query,
    w_keyval,
    w_edge_kv,
    w_out,
    w_move,
    w_trans_in,
    w_trans_out,
    w_gate,
    w_feat_in,
    w_feat_out,
):
    col_count = lax.axis_size("col")
    row_index = lax.axis_index("row")
    col_index = lax.axis_index("col")
    row_count, tile_width, channels = pair.shape
    block_size = row_count // col_count
    own_lists = lax.dynamic_slice_in_dim(neighbours, col_index * block_size, block_size, 0)
    flat_lists = own_lists.reshape(-1)
    tile_owner = flat_lists // tile_width
    outgoing = pair.reshape(col_count, block_size, tile_width, channels)
    received = lax.all_to_all(outgoing, "col", split_axis=0, concat_axis=0, tiled=True)
    local_row = jnp.repeat(jnp.arange(block_size, dtype=jnp.int32), K)
    place_index = (tile_owner * block_size + local_row) * tile_width + flat_lists % tile_width
    edge_in = received.reshape(-1, channels)[place_index]
    states_all, coords_all = (
        lax.all_gather(node_state.astype(jnp.float32), ("row", "col"), axis=0, tiled=True),
        lax.all_gather(coords, ("row", "col"), axis=2, tiled=True),
    )
    keyval_all = jnp.dot(
        states_all.astype(jnp.bfloat16), w_keyval, preferred_element_type=jnp.float32
    ).astype(jnp.bfloat16)
    node_out, coords_new = edge_layer(
        edge_in,
        flat_lists,
        node_state,
        coords,
        keyval_all,
        coords_all,
        w_edge,
        w_radial,
        w_query,
        w_edge_kv,
        w_out,
        w_move,
    )
    moved_all = lax.all_gather(coords_new, ("row", "col"), axis=2, tiled=True)
    row_start = row_index * row_count
    col_start = col_index * tile_width
    row_x = lax.dynamic_slice_in_dim(moved_all, row_start, row_count, 2)
    col_x = lax.dynamic_slice_in_dim(moved_all, col_start, tile_width, 2)
    row_chain = lax.dynamic_slice_in_dim(chain, row_start, row_count, 0)
    col_chain = lax.dynamic_slice_in_dim(chain, col_start, tile_width, 0)
    row_pos = row_start + jnp.arange(row_count, dtype=jnp.int32)
    col_pos = col_start + jnp.arange(tile_width, dtype=jnp.int32)
    features = pair_features(row_x, col_x, row_chain, col_chain, row_pos, col_pos)
    pair_out = pair_update(pair, features, w_trans_in, w_trans_out, w_gate, w_feat_in, w_feat_out)
    return (pair_out, node_out, coords_new)


def solution(mesh):
    in_specs = (
        P("row", "col", None),
        P(("row", "col"), None),
        P(None, None, ("row", "col")),
        P("row", None),
        P(),
        P(),
        P(),
        P(),
        P(),
        P(),
        P(),
        P(),
        P(),
        P(),
        P(),
        P(),
        P(),
    )
    out_specs = (P("row", "col", None), P(("row", "col"), None), P(None, None, ("row", "col")))
    return jax.shard_map(local, mesh=mesh, in_specs=in_specs, out_specs=out_specs, check_vma=False)
```

profile of v0, /device:TPU:1, one launch (start us, length us, event | category | flops | bytes accessed | tf_op | source)
XLA Modules:
  0.0 454.2 jit_solution(16938790472097172447)
XLA Ops:
  0.6 0.0 copy-start
  0.6 7.8 %all-to-all-start = ((bf16[16,16,128,128]{3,2,1,0:T(8,128)(2,1)}), bf16[16,16,128,128]{3,2,1,0:T(8,128)(2,1)}, u32[]{:S(2)}, u32[]{:S(2)}) async-start(bf16[16,16,128,128]{3,2,1,0:T(8,128)(2,1)} %bitcast.94), calls=%async_computation | async-start | bytes 16777216 | tf_op jit(solution)/shard_map/all_to_all | solution.py:157
  8.5 0.0 copy-start.3
  8.5 0.0 copy-start.6
  8.5 5.7 %convert_reduce_fusion = f32[256,128]{1,0:T(8,128)S(1)} fusion(bf16[256,128,128]{2,1,0:T(8,128)(2,1)} %param.17), kind=kLoop, calls=%fused_computation.18 | loop fusion | flops 8355840 | bytes 8519680 | tf_op jit(solution)/shard_map/reduce_sum | solution.py:104
  14.2 0.8 dynamic_slice.19
  14.9 0.8 dynamic_slice.18
  15.7 0.1 reshape.515
  15.8 0.1 constant_dynamic-slice_fusion.6
  15.9 0.1 copy.45
  15.9 0.1 reshape.514
  16.0 0.1 compare_select_fusion
  16.1 0.1 copy.51
  16.2 188.0 %all_gather.10 = bf16[2048,64]{1,0:T(8,128)(2,1)S(1)} all-gather(bf16[16,64]{1,0:T(8,128)(2,1)S(1)} %copy-done.3), channel_id=1, replica_groups=mesh['row'=8,'col'=16] {'row','col'}, dimensions={0}, use_global_device_ids=true | all-gather | bytes 264192 | tf_op jit(solution)/shard_map/all_gather | solution.py:162
  204.2 0.2 fusion.35
  204.4 10.7 %multiply_reduce_fusion = f32[256,128]{1,0:T(8,128)S(1)} fusion(bf16[256,128,128]{2,1,0:T(8,128)(2,1)} %param.17, f32[256,128]{1,0:T(8,128)S(1)} %get-tuple-element.28), kind=kLoop, calls=%fused_computation.17 | loop fusion | flops 16744448 | bytes 8650752 | tf_op jit(solution)/shard_map/reduce_sum | solution.py:107
  215.1 0.2 broadcast_in_dim.8
  215.3 0.2 reshape.518
  215.5 0.3 convolution_convert_fusion
  215.8 3.2 gather_fusion.2
  219.0 0.1 copy.49
  219.2 73.8 %all_gather.9 = f32[3,3,2048]{1,0,2:T(4,128)} all-gather(f32[3,3,16]{1,0,2:T(4,128)S(1)} %copy.51), channel_id=1, replica_groups=mesh['row'=8,'col'=16] {'row','col'}, dimensions={2}, use_global_device_ids=true | all-gather | bytes 74304 | tf_op jit(solution)/shard_map/all_gather | solution.py:163
  293.0 5.7 %gather_fusion.1 = f32[1024,3,3]{2,1,0:T(4,128)S(1)} fusion(f32[3,3,2048]{1,0,2:T(4,128)} %all_gather.9, s32[1024]{0:T(1024)S(1)} %broadcast_clamp_fusion), kind=kCustom, calls=%fused_computation.1 | custom fusion | bytes 77824 | tf_op jit(solution)/shard_map/gather | solution.py:42
  298.8 0.3 broadcast_in_dim.7
  299.1 2.8 fusion.10
  301.9 0.1 eq.32
  302.0 0.8 convert_convert_fusion
  302.8 11.0 %fusion.7 = bf16[32768,128]{1,0:T(8,128)(2,1)S(1)} fusion(bf16[256,128,128]{2,1,0:T(8,128)(2,1)} %param.17, f32[32768]{0:T(1024)S(1)} %rsqrt_bitcast_fusion, f32[32768]{0:T(1024)S(1)} %get-tuple-element.27), kind=kLoop, calls=%fused_computation.15 | loop fusion | flops 16777216 | bytes 17039360 | tf_op jit(solution)/shard_map/convert_element_type | solution.py:108
  313.9 0.0 copy-start.9
  313.9 0.0 copy-start.13
  313.9 8.2 %fusion.5 = f32[32768,128]{1,0:T(8,128)} fusion(bf16[32768,128]{1,0:T(8,128)(2,1)S(1)} %fusion.7, bf16[128,128]{1,0:T(8,128)(2,1)S(1)} %copy-done.12), kind=kOutput, calls=%fused_computation.12 | convolution fusion | flops 1086324736 | bytes 25198592 | tf_op jit(solution)/shard_map/dot_general | solution.py:113
  322.1 1.0 fusion.17
  323.1 0.1 sub.146
  323.2 1.0 multiply_convert_fusion.2
  324.2 7.3 %gather_fusion = bf16[1024,128]{1,0:T(8,128)(2,1)S(1)} fusion(bf16[32768,128]{1,0:T(8,128)(2,1)} %bitcast.4, s32[1024]{0:T(1024)S(1)} %broadcast_clamp_fusion.1), kind=kCustom, calls=%fused_computation | custom fusion | bytes 528384 | tf_op jit(solution)/shard_map/gather | solution.py:160
  331.6 1.2 multiply_convert_fusion.1
  332.8 0.1 fusion.34
  333.0 0.3 fusion.36
  333.3 0.1 bitcast_reduce_fusion
  333.4 0.2 copy.64
  333.7 0.0 copy-start.7
  333.7 1.2 multiply_reduce_fusion.1
  335.0 0.7 copy.62
  335.6 67.9 %all_gather.11 = f32[3,3,2048]{1,0,2:T(4,128)S(1)} all-gather(f32[3,3,16]{1,0,2:T(4,128)S(1)} %add.193), channel_id=1, replica_groups=mesh['row'=8,'col'=16] {'row','col'}, dimensions={2}, use_global_device_ids=true | all-gather | bytes 74304 | tf_op jit(solution)/shard_map/all_gather | solution.py:182
  403.6 0.2 constant_dynamic-slice_fusion.2
  403.7 0.3 constant_dynamic-slice_fusion
  404.1 0.1 mul.240
  404.3 0.9 reshape.521
  405.2 0.1 copy.53
  405.3 0.1 copy.60
  405.4 0.1 copy.55
  405.5 0.1 copy.57
  405.6 0.1 copy.61
  405.7 0.1 copy.58
  405.8 0.4 fusion.15
  406.2 0.1 fusion.24
  406.3 1.0 exponential_convert_fusion
  407.3 1.3 multiply_reduce_fusion.2
  408.5 0.8 convolution_add_fusion.2
  409.3 0.2 copy_bitcast_fusion
  409.5 0.2 copy_bitcast_fusion.2
  409.7 13.4 %concatenate.5 = bf16[42,32768]{1,0:T(8,128)(2,1)} concatenate(bf16[36,32768]{1,0:T(8,128)(2,1)S(1)} %exponential_convert_fusion, bf16[1,32768]{1,0:T(2,128)(2,1)S(1)} %get-tuple-element.36, bf16[1,32768]{1,0:T(2,128)(2,1)S(1)} %get-tuple-element.35, bf16[1,32768]{1,0:T(2,128)(2,1)S(1)} %get-tuple-element.34, bf16[1,32768]{1,0:T(2,128)(2,1)S(1)} %get-tuple-element.33, ...), dimensions={0} | concatenate | bytes 5505024 | tf_op jit(solution)/shard_map/concatenate | solution.py:98
  423.1 12.7 %convolution_multiply_fusion = f32[32768,128]{1,0:T(8,128)} fusion(f32[32768,128]{1,0:T(8,128)} %fusion.5, bf16[128,128]{1,0:T(8,128)(2,1)} %param.33, bf16[42,32768]{1,0:T(8,128)(2,1)} %concatenate.5, bf16[42,128]{1,0:T(8,128)(2,1)S(1)} %copy-done.14), kind=kOutput, calls=%fused_computation.11 | convolution fusion | flops 1451229184 | bytes 36350464 | tf_op jit(solution)/shard_map/dot_general | solution.py:121
  435.8 18.4 %fusion.3 = bf16[32768,128]{1,0:T(8,128)(2,1)} fusion(f32[32768,128]{1,0:T(8,128)} %convolution_multiply_fusion, bf16[256,128]{1,0:T(8,128)(2,1)S(1)} %copy-done, bf16[32768,128]{1,0:T(8,128)(2,1)} %copy-done.1, bf16[128,256]{1,0:T(8,128)(2,1)S(1)} %copy-done.2, bf16[32768,128]{1,0:T(8,128)(2,1)} %bitcast.95), kind=kOutput, calls=%fused_computation.9 | convolution fusion | flops 4328521728 | bytes 42074112 | tf_op jit(solution)/shard_map/dot_general | solution.py:112
  (46 shorter events, 0.4 us)
Async XLA Ops:
  0.6 435.2 %copy-start = (bf16[256,128]{1,0:T(8,128)(2,1)S(1)}, bf16[256,128]{1,0:T(8,128)(2,1)}, u32[]{:S(2)}) copy-start(bf16[256,128]{1,0:T(8,128)(2,1)} %param.30) | copy-start | bytes 196612
  0.6 323.6 %all-to-all-start = ((bf16[16,16,128,128]{3,2,1,0:T(8,128)(2,1)}), bf16[16,16,128,128]{3,2,1,0:T(8,128)(2,1)}, u32[]{:S(2)}, u32[]{:S(2)}) async-start(bf16[16,16,128,128]{3,2,1,0:T(8,128)(2,1)} %bitcast.94), calls=%async_computation | async-start | bytes 16777216 | tf_op jit(solution)/shard_map/all_to_all | solution.py:157
  8.4 7.4 %copy-start.5 = (s32[256,64]{0,1:T(8,128)S(1)}, s32[256,64]{0,1:T(8,128)}, u32[]{:S(2)}) copy-start(s32[256,64]{0,1:T(8,128)} %param.20) | copy-start | bytes 196612
  8.4 7.6 %copy-start.10 = (f32[3,3,16]{2,1,0:T(4,128)S(1)}, f32[3,3,16]{2,1,0:T(4,128)}, u32[]{:S(2)}) copy-start(f32[3,3,16]{2,1,0:T(4,128)} %param.19) | copy-start | bytes 1732
  8.5 7.7 %copy-start.3 = (bf16[16,64]{1,0:T(8,128)(2,1)S(1)}, bf16[16,64]{1,0:T(8,128)(2,1)}, u32[]{:S(2)}) copy-start(bf16[16,64]{1,0:T(8,128)(2,1)} %param.18) | copy-start | bytes 6148
  8.5 195.7 %copy-start.6 = (bf16[64,64]{1,0:T(8,128)(2,1)S(1)}, bf16[64,64]{1,0:T(8,128)(2,1)}, u32[]{:S(2)}) copy-start(bf16[64,64]{1,0:T(8,128)(2,1)} %param.24) | copy-start | bytes 24580
  8.5 207.0 %copy-start.4 = (bf16[64,128]{1,0:T(8,128)(2,1)S(1)}, bf16[64,128]{1,0:T(8,128)(2,1)}, u32[]{:S(2)}) copy-start(bf16[64,128]{1,0:T(8,128)(2,1)} %param.25) | copy-start | bytes 49156
  302.8 11.0 %copy-start.12 = (bf16[128,128]{1,0:T(8,128)(2,1)S(1)}, bf16[128,128]{1,0:T(8,128)(2,1)}, u32[]{:S(2)}) copy-start(bf16[128,128]{1,0:T(8,128)(2,1)} %param.31) | copy-start | bytes 98308
  313.9 8.2 %copy-start.1 = (bf16[32768,128]{1,0:T(8,128)(2,1)}, bf16[32768,128]{1,0:T(8,128)(2,1)S(1)}, u32[]{:S(2)}) copy-start(bf16[32768,128]{1,0:T(8,128)(2,1)S(1)} %fusion.7) | copy-start | bytes 25165828
  313.9 8.2 %copy-start.9 = (bf16[36,64]{1,0:T(8,128)(2,1)S(1)}, bf16[36,64]{1,0:T(8,128)(2,1)}, u32[]{:S(2)}) copy-start(bf16[36,64]{1,0:T(8,128)(2,1)} %param.23) | copy-start | bytes 13828
  313.9 17.7 %copy-start.13 = (bf16[128,64]{0,1:T(8,128)(2,1)S(1)}, bf16[128,64]{0,1:T(8,128)(2,1)}, u32[]{:S(2)}) copy-start(bf16[128,64]{0,1:T(8,128)(2,1)} %param.22) | copy-start | bytes 49156
  313.9 18.9 %copy-start.11 = (bf16[64,12]{0,1:T(8,128)(2,1)S(1)}, bf16[64,12]{0,1:T(8,128)(2,1)}, u32[]{:S(2)}) copy-start(bf16[64,12]{0,1:T(8,128)(2,1)} %param.28) | copy-start | bytes 4612
  313.9 19.0 %copy-start.8 = (bf16[64,128]{1,0:T(8,128)(2,1)S(1)}, bf16[64,128]{1,0:T(8,128)(2,1)}, u32[]{:S(2)}) copy-start(bf16[64,128]{1,0:T(8,128)(2,1)} %param.26) | copy-start | bytes 49156
  333.7 74.8 %copy-start.7 = (bf16[64,64]{1,0:T(8,128)(2,1)S(1)}, bf16[64,64]{1,0:T(8,128)(2,1)}, u32[]{:S(2)}) copy-start(bf16[64,64]{1,0:T(8,128)(2,1)} %param.27) | copy-start | bytes 24580
  404.1 19.0 %copy-start.14 = (bf16[42,128]{1,0:T(8,128)(2,1)S(1)}, bf16[42,128]{1,0:T(8,128)(2,1)}, u32[]{:S(2)}) copy-start(bf16[42,128]{1,0:T(8,128)(2,1)} %param.32) | copy-start | bytes 32260
  423.1 12.7 %copy-start.2 = (bf16[128,256]{1,0:T(8,128)(2,1)S(1)}, bf16[128,256]{1,0:T(8,128)(2,1)}, u32[]{:S(2)}) copy-start(bf16[128,256]{1,0:T(8,128)(2,1)} %param.29) | copy-start | bytes 196612
where the time goes:
time: 455 us; the launch traced here: 454 us
  blocking collectives  330 us (73%)
  matrix products  43 us (9%)
  other arithmetic  36.5 us (8%)
  local copies, waits for them, and re-layouts  36.1 us (8%)
  starting transfers between devices  7.78 us (2%)
    all_gather x1, blocking collectives, local(): lax.all_gather(node_state.astype(jnp.float32), ('row', 'col'), axis=0, ti...  188 us
    all_gather x1, blocking collectives, local(): lax.all_gather(coords, ('row', 'col'), axis=2, tiled=True)  73.8 us
    all_gather x1, blocking collectives, local(): moved_all = lax.all_gather(coords_new, ('row', 'col'), axis=2, tiled=True)  67.9 us
    dot_general x1, matrix products, pair_update(): jnp.dot(trans_hidden, w_trans_out, preferred_element_type=jnp.float32)  18.4 us
    concatenate x1, local copies, waits for them, and re-layouts, pair_features(): jnp.concatenate([radial_basis(distance), tail_feats], axis=0)  13.4 us
    dot_general x1, matrix products, pair_update(): jnp.dot(feat_hidden, w_feat_out, preferred_element_type=jnp.float32)  12.7 us
    convert_element_type x1, other arithmetic, pair_update(): normed = (centred * lax.rsqrt(jnp.mean(centred * centred, axis=1, keepdim...  11 us
    reduce_sum x1, other arithmetic, pair_update(): jnp.mean(centred * centred, axis=1, keepdims=True) + 1e-05  10.7 us
  transfers between devices with their start and end apart: 1, of which 0 were waited for; matrix products, arithmetic and copies ran while one was open for 12% of the time, Pallas kernels for 0%

commit v1 on v0

v1 whole, which is shorter than its diff:
```python
import functools

import jax
import jax.numpy as jnp
from jax import lax
from jax.experimental import pallas as pl
from jax.experimental.pallas import tpu as pltpu
from jax.sharding import PartitionSpec as P

K = 64
NRBF = 36
BOTH = ("row", "col")
F32 = jnp.float32
BF16 = jnp.bfloat16
CENTRE_STEP = 12.0 / 35.0
PIECES = 64
GROUP = 16
SLOTS = 128
GROUPS_PER_STEP = 4
VMEM_LIMIT = 48 * 1024 * 1024


def iota(shape, dim):
    return lax.broadcasted_iota(jnp.int32, shape, dim)


def dot(a, b):
    return jnp.dot(a, b, preferred_element_type=F32)


def dot_t(a, b):
    return lax.dot_general(a, b, (((0,), (0,)), ((), ())), preferred_element_type=F32)


def dot_nt(a, b):
    return lax.dot_general(a, b, (((1,), (1,)), ((), ())), preferred_element_type=F32)


def split2(v):
    high = v.astype(BF16)
    low = (v - high.astype(F32)).astype(BF16)
    return jnp.concatenate([high, low], axis=1)


def sigmoid(v):
    return 0.5 * jnp.tanh(0.5 * v) + 0.5


def silu(v):
    half = 0.5 * v
    return half + half * jnp.tanh(half)


def record_kernel(node_ref, coords_ref, out_ref, parts_ref):
    parts_ref[...] = jnp.zeros_like(parts_ref)
    for a in range(3):
        value = coords_ref[a]
        high = value.astype(BF16).astype(F32)
        rest = value - high
        mid = rest.astype(BF16).astype(F32)
        parts_ref[pl.ds(PIECES + 3 * a, 3), :] = high
        parts_ref[pl.ds(PIECES + 16 + 3 * a, 3), :] = mid
        parts_ref[pl.ds(PIECES + 32 + 3 * a, 3), :] = rest - mid
    eye = (iota((GROUP, GROUP), 0) == iota((GROUP, GROUP), 1)).astype(F32).astype(BF16)
    widen = (iota((64, 128), 0) == iota((64, 128), 1)).astype(F32).astype(BF16)
    record = dot(node_ref[...], widen) + dot_nt(eye, parts_ref[...].astype(BF16))
    out_ref[...] = jnp.broadcast_to(record.astype(BF16)[None], out_ref.shape)


def records(node_state, coords, copies):
    return pl.pallas_call(
        record_kernel,
        out_shape=jax.ShapeDtypeStruct((copies, GROUP, 128), BF16),
        scratch_shapes=[pltpu.VMEM((128, GROUP), F32)],
        name="records",
    )(node_state, coords)


def select_kernel(place_ref, lists_ref, pair_ref, w_edge_ref, out_ref, where_ref, w_ref):
    @pl.when(pl.program_id(0) == 0)
    def _():
        spot = iota((GROUP * 128, 128), 0)
        lane = iota((GROUP * 128, 128), 1)
        column = (jnp.bitwise_and(spot, 127) + 1).astype(F32)
        residue = (lax.shift_right_logical(spot, 7) + 1).astype(F32)
        where_ref[...] = jnp.where(lane == 64, column, jnp.where(lane == 65, residue, 0.0)).astype(BF16)
        widen = (iota((64, 128), 0) == iota((64, 128), 1)).astype(F32).astype(BF16)
        w_ref[...] = dot(w_edge_ref[...], widen).astype(BF16)

    start = place_ref[1] * 128
    lists = (lists_ref[...] - start).astype(F32)
    lists = jnp.concatenate([lists, jnp.full((GROUP, 64), -1.0, F32)], axis=1)
    by_slot = jnp.transpose(lists)
    column = iota((K, 128), 1).astype(F32)
    rows = []
    for i in range(GROUP):
        hit = by_slot[:K, i : i + 1] == column
        rows.append(jnp.sum(jnp.where(hit, 1.0, 0.0), axis=0, keepdims=True))
    chosen = jnp.concatenate(rows, axis=0)
    chosen_b = chosen.astype(BF16)
    before = (iota((128, 128), 0) < iota((128, 128), 1)).astype(F32).astype(BF16)
    earlier = (iota((GROUP, GROUP), 0) > iota((GROUP, GROUP), 1)).astype(F32).astype(BF16)
    totals = dot(chosen_b, jnp.ones((128, 128), BF16))
    rank = dot(chosen_b, before) + dot(earlier, totals.astype(BF16))
    rank = jnp.where(chosen > 0.0, rank, -1.0)
    slot = iota((SLOTS, 128), 0).astype(F32)
    picks = [jnp.where(slot == rank[i : i + 1, :], 1.0, 0.0).astype(BF16) for i in range(GROUP)]
    pick = jnp.concatenate(picks, axis=1)
    found = dot(pick, pair_ref[...].reshape(GROUP * 128, 128))
    marks = dot(pick, where_ref[...])
    out_ref[...] = dot(found.astype(BF16), w_ref[...]) + marks


def select_edges(place, neighbours, pair, w_edge):
    groups = pair.shape[0] // GROUP
    return pl.pallas_call(
        select_kernel,
        grid_spec=pltpu.PrefetchScalarGridSpec(
            num_scalar_prefetch=1,
            grid=(groups,),
            in_specs=[
                pl.BlockSpec((GROUP, K), lambda g, place: (g, 0)),
                pl.BlockSpec((GROUP, 128, 128), lambda g, place: (g, 0, 0)),
                pl.BlockSpec((128, 64), lambda g, place: (0, 0)),
            ],
            out_specs=pl.BlockSpec((SLOTS, 128), lambda g, place: (g, 0)),
            scratch_shapes=[pltpu.VMEM((GROUP * 128, 128), BF16), pltpu.VMEM((128, 128), BF16)],
        ),
        out_shape=jax.ShapeDtypeStruct((groups * SLOTS, 128), F32),
        compiler_params=pltpu.CompilerParams(vmem_limit_bytes=VMEM_LIMIT),
        cost_estimate=pl.CostEstimate(flops=3_000_000_000, bytes_accessed=9 * 2**20, transcendentals=0),
        name="select_edges",
    )(place, neighbours, pair, w_edge)


def edge_kernel(
    place_ref,
    edges_ref,
    cols_ref,
    rows_ref,
    w_radial_ref,
    w_query_ref,
    w_keyval_ref,
    w_edge_kv_ref,
    w_move_ref,
    out_ref,
    w_keyval_s,
    w_query_s,
    w_radial_s,
    w_mix_s,
):
    for ref in (w_keyval_s, w_query_s, w_radial_s, w_mix_s):
        ref[...] = jnp.zeros_like(ref)
    w_keyval_s[0:64, :] = w_keyval_ref[...]
    w_query_s[0:64, 0:64] = w_query_ref[...]
    w_radial_s[0:36, 0:64] = w_radial_ref[...]
    w_mix_s[0:64, 0:128] = w_edge_kv_ref[...]
    w_mix_s[0:64, 128:140] = w_move_ref[...]
    cols = cols_ref[...]
    keyval = dot(cols, w_keyval_s[...]).astype(BF16)
    by_column = jnp.concatenate([keyval, cols], axis=1)
    lane = iota((1, 128), 1)
    source = iota((256, 256), 0)
    target = iota((256, 256), 1)
    channel = jnp.bitwise_and(source, 127)
    head = lax.shift_right_logical(channel, 4)
    for_value = (target >= 64) & (target < 128) & (lax.shift_right_logical(target - 64, 4) == head)
    for_move = (target >= 128) & (target < 140) & (jnp.bitwise_and(target, 3) == head)
    heads = jnp.where((channel < 64) & (for_value | for_move), 0.125, 0.0).astype(BF16)
    source = jnp.bitwise_and(iota((256, 128), 0), 127)
    target = iota((256, 128), 1) - PIECES
    low_atom = lax.shift_right_logical(source, 2) * 3
    spread = jnp.where(
        (source < 12) & (target >= low_atom) & (target < low_atom + 3), 1.0, 0.0
    ).astype(BF16)
    centre = lane.astype(F32) * CENTRE_STEP
    alpha = jnp.where((lane >= PIECES + 3) & (lane < PIECES + 6), 1.0, 0.0)
    per = GROUPS_PER_STEP * SLOTS
    own = GROUPS_PER_STEP * GROUP
    steps = edges_ref.shape[0] // per
    lane_f = lane.astype(F32)
    shift_by = lax.shift_right_logical(iota((per, 128), 0), 7) * GROUP
    parts = []
    for step in range(steps):
        edges = edges_ref[pl.ds(step * per, per), :]
        column = edges[:, 64:65] - 1.0
        residue = edges[:, 65:66] - 1.0
        pick_col = jnp.where(column == lane_f, 1.0, 0.0).astype(BF16)
        target_row = jnp.where((lane >= shift_by) & (lane < shift_by + GROUP), lane - shift_by, -2).astype(F32)
        pick_row = jnp.where(residue == target_row, 1.0, 0.0).astype(BF16)
        rows = rows_ref[pl.ds(step * own, own), :]
        rows = jnp.concatenate([rows, jnp.zeros((128 - own, 128), BF16)], axis=0)
        from_col = dot(pick_col, by_column)
        from_row = dot(pick_row, rows)
        gap = from_col[:, 128:] - from_row
        relative = gap + pltpu.roll(gap, 112, 1) + pltpu.roll(gap, 96, 1)
        distance = jnp.sqrt(jnp.sum(relative * relative * alpha, axis=1, keepdims=True))
        offset = (distance - centre) * 2.0
        basis = jnp.exp(-(offset * offset)).astype(BF16)
        hidden = silu(edges + dot(basis, w_radial_s[...])).astype(BF16)
        mix = dot(hidden, w_mix_s[...])
        keyval_edge = from_col[:, :128] + mix[:, :128]
        queries = dot(from_row.astype(BF16), w_query_s[...])
        attention = 0.5 * jnp.tanh(dot(split2(queries * keyval_edge), heads)) + 0.5
        values = attention[:, :128] * keyval_edge
        moves = attention[:, 128:] * mix[:, 128:]
        move = dot(split2(moves), spread) * relative
        both = jnp.where(lane < 64, pltpu.roll(move, 64, 1), values)
        summed = dot_t(pick_row, split2(both))
        parts.append((summed[:own, :128] + summed[:own, 128:]) * (1.0 / K))
    total = jnp.concatenate(parts, axis=0)
    atoms = rows_ref[...].astype(F32)
    atoms = atoms + pltpu.roll(atoms, 112, 1) + pltpu.roll(atoms, 96, 1)
    first = jnp.where(place_ref[1] == 0, 1.0, 0.0)
    total = total + jnp.where(lane < 9, pltpu.roll(atoms, 64, 1), 0.0) * first
    by_lane = jnp.transpose(total)
    groups = out_ref.shape[0]
    for d in range(groups):
        out_ref[d, 0:16, :] = total[d * GROUP : (d + 1) * GROUP, :]
        out_ref[d, 16:24, :] = by_lane[0:8, 0:128]
        out_ref[d, 24:32, :] = by_lane[0:8, 128:256]
        out_ref[d, 32:40, :] = jnp.concatenate(
            [by_lane[8:9, 0:128], by_lane[8:9, 128:256], jnp.zeros((6, 128), F32)], axis=0
        )


def edge_sums(place, edges, table, w_radial, w_query, w_keyval, w_edge_kv, w_move):
    groups = edges.shape[0] // SLOTS
    whole = lambda shape: pl.BlockSpec(shape, lambda i, place: (0,) * len(shape))
    return pl.pallas_call(
        edge_kernel,
        grid_spec=pltpu.PrefetchScalarGridSpec(
            num_scalar_prefetch=1,
            grid=(1,),
            in_specs=[
                whole(edges.shape),
                pl.BlockSpec((128, 128), lambda i, place: (place[1], 0)),
                pl.BlockSpec((256, 128), lambda i, place: (place[0], 0)),
                whole(w_radial.shape),
                whole(w_query.shape),
                whole(w_keyval.shape),
                whole(w_edge_kv.shape),
                whole(w_move.shape),
            ],
            out_specs=whole((groups, 40, 128)),
            scratch_shapes=[
                pltpu.VMEM((128, 128), BF16),
                pltpu.VMEM((128, 128), BF16),
                pltpu.VMEM((128, 128), BF16),
                pltpu.VMEM((128, 256), BF16),
            ],
        ),
        out_shape=jax.ShapeDtypeStruct((groups, 40, 128), F32),
        compiler_params=pltpu.CompilerParams(vmem_limit_bytes=VMEM_LIMIT),
        cost_estimate=pl.CostEstimate(flops=2_000_000_000, bytes_accessed=3 * 2**20, transcendentals=0),
        name="edge_sums",
    )(place, edges, table, table, w_radial, w_query, w_keyval, w_edge_kv, w_move)


def total_kernel(place_ref, parts_ref, node_ref, w_out_ref, node_out_ref, own_ref, rows_ref, send_ref, w_ref):
    col = place_ref[1]
    total = parts_ref[0]
    for d in range(1, parts_ref.shape[0]):
        total = total + parts_ref[d]
    w_ref[...] = jnp.zeros_like(w_ref)
    w_ref[64:128, :] = w_out_ref[...]
    message = total[0:16, :].astype(BF16)
    node_out_ref[...] = node_ref[...].astype(F32) + dot(message, w_ref[...])
    left = jnp.concatenate([total[16:24, :], total[32:33, :], jnp.zeros((7, 128), F32)], axis=0)
    right = jnp.concatenate([total[24:32, :], total[33:34, :], jnp.zeros((7, 128), F32)], axis=0)
    rows_ref[:, 0:128] = left
    rows_ref[:, 128:256] = right
    odd = jnp.bitwise_and(col, 1) == 1
    send_ref[...] = jnp.broadcast_to(jnp.where(odd, right, left)[None], send_ref.shape)
    mine = jnp.where(col >= 8, right, left)
    mine = pltpu.roll(mine, jnp.bitwise_and(128 - jnp.bitwise_and(col, 7) * GROUP, 127), 1)
    for a in range(3):
        own_ref[a] = mine[3 * a : 3 * a + 3, 0:GROUP]


def totals(place, parts, node_state, w_out, copies):
    return pl.pallas_call(
        total_kernel,
        in_specs=[pl.BlockSpec(memory_space=pltpu.SMEM)] + [pl.BlockSpec(memory_space=pltpu.VMEM)] * 3,
        out_shape=[
            jax.ShapeDtypeStruct((GROUP, 64), F32),
            jax.ShapeDtypeStruct((3, 3, GROUP), F32),
            jax.ShapeDtypeStruct((16, 256), F32),
            jax.ShapeDtypeStruct((copies, 16, 128), F32),
        ],
        scratch_shapes=[pltpu.VMEM((128, 64), BF16)],
        name="totals",
    )(place, parts, node_state, w_out)


def transition_kernel(pair_ref, w_in_ref, w_out_ref, w_gate_ref, *refs):
    base_ref, gate_ref = refs[-2:]
    rows = pair_ref.shape[0]
    for i in range(0, rows, 2):
        x = pair_ref[pl.ds(i, 2)].reshape(256, 128).astype(F32)
        centred = x - jnp.mean(x, axis=1, keepdims=True)
        scale = lax.rsqrt(jnp.mean(centred * centred, axis=1, keepdims=True) + 1e-05)
        normed = (centred * scale).astype(BF16)
        hidden = jnp.maximum(dot(normed, w_in_ref[...]), 0.0).astype(BF16)
        gate = sigmoid(dot(normed, w_gate_ref[...]))
        base = x + dot(hidden, w_out_ref[...])
        base_ref[pl.ds(i, 2)] = base.astype(BF16).reshape(2, 128, 128)
        gate_ref[pl.ds(i, 2)] = gate.astype(BF16).reshape(2, 128, 128)


def transition(pair, w_in, w_out, w_gate, first, count, made=None):
    block = 16
    rows = pl.BlockSpec((block, 128, 128), lambda i: (i + first // block, 0, 0))
    whole = lambda a: pl.BlockSpec(a.shape, lambda i: (0,) * a.ndim)
    before = [] if made is None else list(made)
    shape = jax.ShapeDtypeStruct(pair.shape, BF16)
    return pl.pallas_call(
        transition_kernel,
        grid=(count // block,),
        in_specs=[rows, whole(w_in), whole(w_out), whole(w_gate)]
        + [pl.BlockSpec(memory_space=pl.ANY)] * len(before),
        out_specs=[rows, rows],
        out_shape=[shape, shape],
        input_output_aliases={4 + i: i for i in range(len(before))},
        compiler_params=pltpu.CompilerParams(vmem_limit_bytes=VMEM_LIMIT),
        cost_estimate=pl.CostEstimate(
            flops=count * 128 * 2 * 128 * 640, bytes_accessed=count * 128 * 128 * 6, transcendentals=0
        ),
        name="transition",
    )(pair, w_in, w_out, w_gate, *before)


def structure_kernel(
    place_ref,
    rows_ref,
    row_chain_ref,
    cols_ref,
    col_chain_ref,
    base_ref,
    gate_ref,
    w_in_ref,
    w_out_ref,
    out_ref,
    w_in_s,
    w_out_s,
):
    step = pl.program_id(0)

    @pl.when(step == 0)
    def _():
        w_in_s[...] = jnp.zeros_like(w_in_s)
        w_out_s[...] = jnp.zeros_like(w_out_s)
        half = (w_in_ref[...].astype(F32) * 0.5).astype(BF16)
        for k in range(2):
            w_in_s[48 * k : 48 * k + 36, 128 * k : 128 * (k + 1)] = half[0:36]
            w_in_s[48 * k + 40 : 48 * k + 46, 128 * k : 128 * (k + 1)] = half[36:42]
            w_out_s[128 * k : 128 * (k + 1), 128 * k : 128 * (k + 1)] = w_out_ref[...]

    rows = base_ref.shape[0]
    cols = cols_ref[0]
    wide = lambda v: jnp.broadcast_to(v, (8, 128))
    alpha = [wide(cols[3 + x : 4 + x, :]) for x in range(3)]
    feature = iota((8, 128), 0)
    bonds = [
        jnp.where(
            feature == 2,
            alpha[x] - wide(cols[x : x + 1, :]),
            jnp.where(feature == 3, alpha[x] - wide(cols[6 + x : 7 + x, :]), 0.0),
        )
        for x in range(3)
    ]
    chain = wide(col_chain_ref[...])
    position = iota((8, 128), 1) + place_ref[1] * 128
    centre = [(iota((8, 128), 0) + 8 * b).astype(F32) * CENTRE_STEP for b in range(5)]

    def features(row):
        p = [rows_ref[3 + x, row] for x in range(3)]
        rn = [rows_ref[x, row] - p[x] for x in range(3)]
        rc = [rows_ref[6 + x, row] - p[x] for x in range(3)]
        gap = [alpha[x] - p[x] for x in range(3)]
        square = gap[0] * gap[0] + gap[1] * gap[1] + gap[2] * gap[2]
        distance = jnp.sqrt(square)
        inverse = 1.0 / (1.0 + distance)
        vectors = [
            jnp.where(feature == 0, rn[x], jnp.where(feature == 1, rc[x], bonds[x])) for x in range(3)
        ]
        orient = (vectors[0] * gap[0] + vectors[1] * gap[1] + vectors[2] * gap[2]) * inverse
        same = jnp.where(chain == row_chain_ref[row], 1.0, 0.0)
        at = row + place_ref[0] * 256
        offset = same * (jnp.clip(position - at, -32, 32).astype(F32) * (1.0 / 32.0))
        tail = jnp.where(feature == 4, same, jnp.where(feature == 5, offset, orient))
        tail = jnp.where(feature < 6, tail, 0.0)
        basis = []
        for b in range(5):
            t = (distance - centre[b]) * 2.0
            basis.append(jnp.exp(-(t * t)))
        return basis + [tail]

    for i in range(0, rows, 2):
        row = step * rows + i
        feats = jnp.concatenate(features(row) + features(row + 1), axis=0).astype(BF16)
        half = dot_t(feats, w_in_s[...])
        hidden = (half + half * jnp.tanh(half)).astype(BF16)
        term = dot(hidden, w_out_s[...])
        for k in range(2):
            gate = gate_ref[i + k].astype(F32)
            base = base_ref[i + k].astype(F32)
            out_ref[i + k] = (base + gate * term[:, 128 * k : 128 * (k + 1)]).astype(BF16)


def structure(place, rows, row_chain, cols, col_chain, base, gate, w_in, w_out):
    block = 16
    tile = pl.BlockSpec((block, 128, 128), lambda i, place: (i, 0, 0))
    whole = lambda a: pl.BlockSpec(a.shape, lambda i, place: (0,) * a.ndim)
    return pl.pallas_call(
        structure_kernel,
        grid_spec=pltpu.PrefetchScalarGridSpec(
            num_scalar_prefetch=1,
            grid=(base.shape[0] // block,),
            in_specs=[
                pl.BlockSpec(memory_space=pltpu.SMEM),
                pl.BlockSpec(memory_space=pltpu.SMEM),
                pl.BlockSpec((1, 16, 128), lambda i, place: (place[1] // 2, 0, 0)),
                whole(col_chain),
                tile,
                tile,
                whole(w_in),
                whole(w_out),
            ],
            out_specs=tile,
            scratch_shapes=[pltpu.VMEM((96, 256), BF16), pltpu.VMEM((256, 256), BF16)],
        ),
        out_shape=jax.ShapeDtypeStruct(base.shape, BF16),
        compiler_params=pltpu.CompilerParams(vmem_limit_bytes=VMEM_LIMIT),
        name="structure",
    )(place, rows, row_chain, cols, col_chain, base, gate, w_in, w_out)


def exchange(v, axis):
    return lax.all_to_all(v, axis, split_axis=0, concat_axis=0, tiled=True)


def local(
    pair,
    node_state,
    coords,
    neighbours,
    chain,
    w_edge,
    w_radial,
    w_query,
    w_keyval,
    w_edge_kv,
    w_out,
    w_move,
    w_trans_in,
    w_trans_out,
    w_gate,
    w_feat_in,
    w_feat_out,
):
    row_devices = lax.axis_size("row")
    col_devices = lax.axis_size("col")
    row_index = lax.axis_index("row")
    col_index = lax.axis_index("col")
    place = jnp.stack([row_index, col_index]).astype(jnp.int32)
    row_chain = lax.dynamic_slice_in_dim(chain, row_index * 256, 256, 0)
    col_chain = lax.dynamic_slice_in_dim(chain, col_index * 128, 128, 0).reshape(1, 128)

    table = exchange(records(node_state, coords, row_devices * col_devices), BOTH)
    edges = select_edges(place, neighbours, pair, w_edge)
    made = transition(pair, w_trans_in, w_trans_out, w_gate, 0, 32)
    parts = edge_sums(
        place, edges, table.reshape(-1, 128), w_radial, w_query, w_keyval, w_edge_kv, w_move
    )
    held, parts = lax.optimization_barrier((made, parts))
    parts = exchange(parts, "col")
    made = transition(pair, w_trans_in, w_trans_out, w_gate, 32, 128, held)
    node_out, own, rows, send = totals(place, parts, node_state, w_out, row_devices)
    held, send = lax.optimization_barrier((made, send))
    cols = exchange(send, "row")
    base, gate = transition(pair, w_trans_in, w_trans_out, w_gate, 160, 96, held)
    pair_out = structure(place, rows, row_chain, cols, col_chain, base, gate, w_feat_in, w_feat_out)
    return (pair_out, node_out, own)


def solution(mesh):
    spread = P(None, None, BOTH)
    in_specs = (P("row", "col", None), P(BOTH, None), spread, P("row", None)) + (P(),) * 13
    out_specs = (P("row", "col", None), P(BOTH, None), spread)
    return jax.shard_map(local, mesh=mesh, in_specs=in_specs, out_specs=out_specs, check_vma=False)
```

time: 455 us -> 110 us (0.24)
  blocking collectives: 330 us -> 0 us
  Pallas kernels: 0 us -> 76.9 us
  matrix products: 43 us -> 0 us
  other arithmetic: 36.5 us -> 0.07 us
  local copies, waits for them, and re-layouts: 36.1 us -> 7.28 us
  starting transfers between devices: 7.78 us -> 23.6 us
    all_gather x3 -> x0, blocking collectives: 330 us -> none  [the longest x1 188 us: local(): lax.all_gather(node_state.astype(jnp.float32), ('row', 'col'), axis=0, ti...]
    pallas_call x0 -> x8, Pallas kernels: none -> 76.9 us  [the longest x3 28.5 us: transition(): pl.pallas_call(transition_kernel, grid=(count // block,), in_specs=[rows,...]
    dot_general x10 -> x0, matrix products: 43 us -> none  [the longest x1 18.4 us: pair_update(): jnp.dot(trans_hidden, w_trans_out, preferred_element_type=jnp.float32)]
    reduce_sum x8 -> x0, other arithmetic: 22.2 us -> none  [the longest x1 10.7 us: pair_update(): jnp.mean(centred * centred, axis=1, keepdims=True) + 1e-05]
    gather x4 -> x0, local copies, waits for them, and re-layouts: 16.4 us -> none  [the longest x1 7.34 us: local(): edge_in = received.reshape(-1, channels)[place_index]]
    all_to_all x1 -> x3, starting transfers between devices: 7.78 us -> 23.6 us  [exchange(): return lax.all_to_all(v, axis, split_axis=0, concat_axis=0, tiled=True)]
    concatenate x1 -> x0, local copies, waits for them, and re-layouts: 13.4 us -> none  [pair_features(): jnp.concatenate([radial_basis(distance), tail_feats], axis=0)]
    convert_element_type x2 -> x0, other arithmetic: 11.1 us -> none  [the longest x1 11 us: pair_update(): normed = (centred * lax.rsqrt(jnp.mean(centred * centred, axis=1, keepdim...]
  transfers between devices with their start and end apart: 1 -> 3, of which waited for: 0 -> 0; matrix products, arithmetic and copies ran while one was open for 12% -> 4% of each run, Pallas kernels for 0% -> 44%
where the time goes in v1:
time: 110 us; the launch traced here: 109 us
  Pallas kernels  76.9 us (70%)
  starting transfers between devices  23.6 us (21%)
  local copies, waits for them, and re-layouts  7.28 us (7%)
    pallas_call x3, Pallas kernels, transition(): pl.pallas_call(transition_kernel, grid=(count // block,), in_specs=[rows,...  28.5 us
    all_to_all x3, starting transfers between devices, exchange(): return lax.all_to_all(v, axis, split_axis=0, concat_axis=0, tiled=True)  23.6 us
    pallas_call x1, Pallas kernels, select_edges(): pl.pallas_call(select_kernel, grid_spec=pltpu.PrefetchScalarGridSpec(num_...  19.5 us
    pallas_call x1, Pallas kernels, structure(): pl.pallas_call(structure_kernel, grid_spec=pltpu.PrefetchScalarGridSpec(n...  18.7 us
    pallas_call x1, Pallas kernels, edge_sums(): pl.pallas_call(edge_kernel, grid_spec=pltpu.PrefetchScalarGridSpec(num_sc...  6.75 us
    unnamed x35, local copies, waits for them, and re-layouts  5.76 us
  transfers between devices with their start and end apart: 3, of which 0 were waited for; matrix products, arithmetic and copies ran while one was open for 4% of the time, Pallas kernels for 44%

profile of v1, /device:TPU:1, one launch (start us, length us, event | category | flops | bytes accessed | tf_op | source)
XLA Modules:
  0.0 108.6 jit_solution(12691312533834133495)
XLA Ops:
  0.6 1.7 %records.1 = bf16[128,16,128]{2,1,0:T(8,128)(2,1)} custom-call(bf16[16,64]{1,0:T(8,128)(2,1)} %node_ref.3, f32[3,3,16]{2,1,0:T(4,128)} %coords_ref.1), custom_call_target="tpu_custom_call" | custom-call | tf_op jit(solution)/shard_map/records/pallas_call | solution.py:71
  2.3 11.5 %all-to-all-start = ((bf16[128,16,128]{2,1,0:T(8,128)(2,1)}), bf16[128,16,128]{2,1,0:T(8,128)(2,1)S(1)}, u32[]{:S(2)}, u32[]{:S(2)}) async-start(bf16[128,16,128]{2,1,0:T(8,128)(2,1)} %records.1), calls=%async_computation | async-start | bytes 1048576 | tf_op jit(solution)/shard_map/all_to_all | solution.py:440
  13.8 0.8 copy.26.w_move_ref
  14.6 0.8 copy.25.w_edge_ref
  15.5 0.9 copy.24.lists_ref
  16.4 0.0 copy-start
  16.4 0.8 copy-done
  17.2 0.0 copy-start.2
  17.2 0.8 copy-done.2
  18.1 0.0 copy-start.4
  18.1 0.8 copy-done.4
  18.8 0.0 copy-start.11
  18.8 0.0 copy-start.12
  18.8 0.0 copy-start.13
  18.9 0.0 copy-start.14
  18.9 4.8 %transition.3 = (bf16[256,128,128]{2,1,0:T(8,128)(2,1)}, bf16[256,128,128]{2,1,0:T(8,128)(2,1)}) custom-call(bf16[256,128,128]{2,1,0:T(8,128)(2,1)} %pair_ref.7, bf16[128,256]{1,0:T(8,128)(2,1)S(1)} %copy-done, bf16[256,128]{1,0:T(8,128)(2,1)S(1)} %copy-done.2, bf16[128,128]{1,0:T(8,128)(2,1)S(1)} %copy-done.4), custom_call_target="tpu_custom_call" | custom-call | flops 671088640 | bytes 3145728 | tf_op jit(solution)/shard_map/transition/pallas_call | solution.py:317
  23.6 0.1 pad_add_fusion.place_ref
  23.7 0.0 copy-start.9
  23.7 0.0 copy-start.1
  23.7 0.0 copy-start.3
  23.7 0.0 copy-start.5
  23.7 19.5 %select_edges.1.edges_ref = f32[2048,128]{1,0:T(8,128)S(1)} custom-call(s32[2]{0:T(128)S(1)} %pad_add_fusion.place_ref, s32[256,64]{1,0:T(8,128)S(1)} %copy.24.lists_ref, bf16[256,128,128]{2,1,0:T(8,128)(2,1)} %pair_ref.7, bf16[128,64]{1,0:T(8,128)(2,1)S(1)} %copy.25.w_edge_ref), custom_call_target="tpu_custom_call" | custom-call | flops 3000000000 | bytes 9437184 | tf_op jit(solution)/shard_map/select_edges/pallas_call | solution.py:116
  43.2 0.0 all-to-all-done
  43.2 0.0 copy-done.11
  43.3 0.0 copy-done.12
  43.3 0.0 copy-done.13
  43.3 0.0 copy-done.14
  43.3 6.8 %edge_sums.1 = f32[16,40,128]{2,1,0:T(8,128)} custom-call(s32[2]{0:T(128)S(1)} %pad_add_fusion.place_ref, f32[2048,128]{1,0:T(8,128)S(1)} %select_edges.1.edges_ref, bf16[2048,128]{1,0:T(8,128)(2,1)S(1)} %bitcast.5, bf16[2048,128]{1,0:T(8,128)(2,1)S(1)} %bitcast.6, bf16[36,64]{1,0:T(8,128)(2,1)S(1)} %copy-done.14, bf16[64,64]{1,0:T(8,128)(2,1)S(1)} %copy-done.11, ...), custom_call_target="tpu_custom_call" | custom-call | flops 2000000000 | bytes 3145728 | tf_op jit(solution)/shard_map/edge_sums/pallas_call | solution.py:230
  50.0 0.0 copy-done.9
  50.0 6.7 %all-to-all-start.1 = ((f32[16,40,128]{2,1,0:T(8,128)}), f32[16,40,128]{2,1,0:T(8,128)S(1)}, u32[]{:S(2)}, u32[]{:S(2)}) async-start(f32[16,40,128]{2,1,0:T(8,128)} %edge_sums.1), calls=%async_computation.1 | async-start | bytes 655360 | tf_op jit(solution)/shard_map/all_to_all | solution.py:440
  56.7 0.8 dynamic-slice_bitcast_fusion.col_chain_ref
  57.5 0.8 dynamic_slice.6.row_chain_ref
  58.3 0.0 copy-done.1
  58.3 0.0 copy-done.3
  58.3 0.0 copy-done.5
  58.3 13.2 %transition.4 = (bf16[256,128,128]{2,1,0:T(8,128)(2,1)}, bf16[256,128,128]{2,1,0:T(8,128)(2,1)}) custom-call(bf16[256,128,128]{2,1,0:T(8,128)(2,1)} %pair_ref.7, bf16[128,256]{1,0:T(8,128)(2,1)S(1)} %copy-done.1, bf16[256,128]{1,0:T(8,128)(2,1)S(1)} %copy-done.3, bf16[128,128]{1,0:T(8,128)(2,1)S(1)} %copy-done.5, ...), custom_call_target="tpu_custom_call", output_to_operand_aliasing={{0}: (4, {}), {1}: (5, {})} | custom-call | flops 2684354560 | bytes 12582912 | tf_op jit(solution)/shard_map/transition/pallas_call | solution.py:317
  71.5 0.0 all-to-all-done.1.parts_ref
  71.5 0.0 copy-start.15
  71.5 0.7 copy-done.15
  72.2 1.7 %totals.1 = (f32[16,64]{1,0:T(8,128)}, f32[3,3,16]{2,1,0:T(4,128)}, f32[16,256]{1,0:T(8,128)}, f32[8,16,128]{2,1,0:T(8,128)}) custom-call(s32[2]{0:T(128)} %copy-done.9, f32[16,40,128]{2,1,0:T(8,128)} %copy-done.15, bf16[16,64]{1,0:T(8,128)(2,1)} %node_ref.3, bf16[64,64]{1,0:T(8,128)(2,1)} %w_out_ref.6), custom_call_target="tpu_custom_call" | custom-call | tf_op jit(solution)/shard_map/totals/pallas_call | solution.py:282
  74.0 5.4 %all-to-all-start.2 = ((f32[8,16,128]{2,1,0:T(8,128)}), f32[8,16,128]{2,1,0:T(8,128)S(1)}, u32[]{:S(2)}, u32[]{:S(2)}) async-start(f32[8,16,128]{2,1,0:T(8,128)} %get-tuple-element.28), calls=%async_computation.2 | async-start | bytes 131072 | tf_op jit(solution)/shard_map/all_to_all | solution.py:440
  79.4 0.0 copy-start.6
  79.4 0.0 copy-start.7
  79.4 0.0 copy-start.8
  79.4 0.0 copy-start.10
  79.5 10.5 %transition.5 = (bf16[256,128,128]{2,1,0:T(8,128)(2,1)}, bf16[256,128,128]{2,1,0:T(8,128)(2,1)}) custom-call(bf16[256,128,128]{2,1,0:T(8,128)(2,1)} %pair_ref.7, bf16[128,256]{1,0:T(8,128)(2,1)S(1)} %copy-done.1, bf16[256,128]{1,0:T(8,128)(2,1)S(1)} %copy-done.3, bf16[128,128]{1,0:T(8,128)(2,1)S(1)} %copy-done.5, ...), custom_call_target="tpu_custom_call", output_to_operand_aliasing={{0}: (4, {}), {1}: (5, {})} | custom-call | flops 2013265920 | bytes 9437184 | tf_op jit(solution)/shard_map/transition/pallas_call | solution.py:317
  89.9 0.0 all-to-all-done.2.cols_ref
  89.9 0.0 copy-done.6
  89.9 0.0 copy-done.7
  89.9 0.0 copy-done.8
  90.0 0.0 copy-done.10
  90.0 18.7 %structure.1 = bf16[256,128,128]{2,1,0:T(8,128)(2,1)} custom-call(s32[2]{0:T(128)S(1)} %copy-done.10, f32[16,256]{1,0:T(8,128)S(1)} %copy-done.7, s32[256]{0:T(256)S(1)} %dynamic_slice.6.row_chain_ref, f32[8,16,128]{2,1,0:T(8,128)S(1)} %all-to-all-done.2.cols_ref, s32[1,128]{1,0:T(1,128)S(1)} %dynamic-slice_bitcast_fusion.col_chain_ref, ...), custom_call_target="tpu_custom_call" | custom-call | tf_op jit(solution)/shard_map/structure/pallas_call | solution.py:415
Async XLA Ops:
  2.3 40.9 %all-to-all-start = ((bf16[128,16,128]{2,1,0:T(8,128)(2,1)}), bf16[128,16,128]{2,1,0:T(8,128)(2,1)S(1)}, u32[]{:S(2)}, u32[]{:S(2)}) async-start(bf16[128,16,128]{2,1,0:T(8,128)(2,1)} %records.1), calls=%async_computation | async-start | bytes 1048576 | tf_op jit(solution)/shard_map/all_to_all | solution.py:440
  16.4 0.8 copy-start
  17.2 0.8 copy-start.2
  18.1 0.8 copy-start.4
  18.8 24.4 %copy-start.11 = (bf16[64,64]{1,0:T(8,128)(2,1)S(1)}, bf16[64,64]{1,0:T(8,128)(2,1)}, u32[]{:S(2)}) copy-start(bf16[64,64]{1,0:T(8,128)(2,1)} %w_query_ref.1) | copy-start | bytes 24580
  18.8 24.4 %copy-start.12 = (bf16[64,128]{1,0:T(8,128)(2,1)S(1)}, bf16[64,128]{1,0:T(8,128)(2,1)}, u32[]{:S(2)}) copy-start(bf16[64,128]{1,0:T(8,128)(2,1)} %w_keyval_ref.1) | copy-start | bytes 49156
  18.8 24.4 %copy-start.13 = (bf16[64,128]{1,0:T(8,128)(2,1)S(1)}, bf16[64,128]{1,0:T(8,128)(2,1)}, u32[]{:S(2)}) copy-start(bf16[64,128]{1,0:T(8,128)(2,1)} %w_edge_kv_ref.1) | copy-start | bytes 49156
  18.9 24.4 %copy-start.14 = (bf16[36,64]{1,0:T(8,128)(2,1)S(1)}, bf16[36,64]{1,0:T(8,128)(2,1)}, u32[]{:S(2)}) copy-start(bf16[36,64]{1,0:T(8,128)(2,1)} %w_radial_ref.1) | copy-start | bytes 13828
  23.7 26.3 %copy-start.9 = (s32[2]{0:T(128)}, s32[2]{0:T(128)S(1)}, u32[]{:S(2)}) copy-start(s32[2]{0:T(128)S(1)} %pad_add_fusion.place_ref) | copy-start | bytes 28
  23.7 34.6 %copy-start.1 = (bf16[128,256]{1,0:T(8,128)(2,1)S(1)}, bf16[128,256]{1,0:T(8,128)(2,1)}, u32[]{:S(2)}) copy-start(bf16[128,256]{1,0:T(8,128)(2,1)} %w_in_ref.6) | copy-start | bytes 196612
  23.7 34.6 %copy-start.3 = (bf16[256,128]{1,0:T(8,128)(2,1)S(1)}, bf16[256,128]{1,0:T(8,128)(2,1)}, u32[]{:S(2)}) copy-start(bf16[256,128]{1,0:T(8,128)(2,1)} %w_out_ref.8) | copy-start | bytes 196612
  23.7 34.6 %copy-start.5 = (bf16[128,128]{1,0:T(8,128)(2,1)S(1)}, bf16[128,128]{1,0:T(8,128)(2,1)}, u32[]{:S(2)}) copy-start(bf16[128,128]{1,0:T(8,128)(2,1)} %w_gate_ref.5) | copy-start | bytes 98308
  50.0 21.5 %all-to-all-start.1 = ((f32[16,40,128]{2,1,0:T(8,128)}), f32[16,40,128]{2,1,0:T(8,128)S(1)}, u32[]{:S(2)}, u32[]{:S(2)}) async-start(f32[16,40,128]{2,1,0:T(8,128)} %edge_sums.1), calls=%async_computation.1 | async-start | bytes 655360 | tf_op jit(solution)/shard_map/all_to_all | solution.py:440
  71.5 0.7 copy-start.15
  74.0 15.9 %all-to-all-start.2 = ((f32[8,16,128]{2,1,0:T(8,128)}), f32[8,16,128]{2,1,0:T(8,128)S(1)}, u32[]{:S(2)}, u32[]{:S(2)}) async-start(f32[8,16,128]{2,1,0:T(8,128)} %get-tuple-element.28), calls=%async_computation.2 | async-start | bytes 131072 | tf_op jit(solution)/shard_map/all_to_all | solution.py:440
  79.4 10.5 %copy-start.6 = (bf16[128,128]{1,0:T(8,128)(2,1)S(1)}, bf16[128,128]{1,0:T(8,128)(2,1)}, u32[]{:S(2)}) copy-start(bf16[128,128]{1,0:T(8,128)(2,1)} %w_out_ref.9) | copy-start | bytes 98308
  79.4 10.5 %copy-start.7 = (f32[16,256]{1,0:T(8,128)S(1)}, f32[16,256]{1,0:T(8,128)}, u32[]{:S(2)}) copy-start(f32[16,256]{1,0:T(8,128)} %get-tuple-element.22.rows_ref) | copy-start | bytes 49156
  79.4 10.5 %copy-start.8 = (bf16[42,128]{1,0:T(8,128)(2,1)S(1)}, bf16[42,128]{1,0:T(8,128)(2,1)}, u32[]{:S(2)}) copy-start(bf16[42,128]{1,0:T(8,128)(2,1)} %w_in_ref.7) | copy-start | bytes 32260
  79.4 10.5 %copy-start.10 = (s32[2]{0:T(128)S(1)}, s32[2]{0:T(128)}, u32[]{:S(2)}) copy-start(s32[2]{0:T(128)} %copy-done.9) | copy-start | bytes 28

commit v2 on v1

v2 whole, which is shorter than its diff:
```python
import functools

import jax
import jax.numpy as jnp
from jax import lax
from jax.experimental import pallas as pl
from jax.experimental.pallas import tpu as pltpu
from jax.sharding import PartitionSpec as P

K = 64
NRBF = 36
BOTH = ("row", "col")
F32 = jnp.float32
BF16 = jnp.bfloat16
CENTRE_STEP = 12.0 / 35.0
PIECES = 64
GROUP = 16
SLOTS = 128
GROUPS_PER_STEP = 4
VMEM_LIMIT = 48 * 1024 * 1024
SMALL_LIMIT = 8 * 1024 * 1024
BLOCK = 32
FIRST = 96
SECOND = 64


def iota(shape, dim):
    return lax.broadcasted_iota(jnp.int32, shape, dim)


def dot(a, b):
    return jnp.dot(a, b, preferred_element_type=F32)


def dot_t(a, b):
    return lax.dot_general(a, b, (((0,), (0,)), ((), ())), preferred_element_type=F32)


def dot_nt(a, b):
    return lax.dot_general(a, b, (((1,), (1,)), ((), ())), preferred_element_type=F32)


def split2(v):
    high = v.astype(BF16)
    low = (v - high.astype(F32)).astype(BF16)
    return jnp.concatenate([high, low], axis=1)


def sigmoid(v):
    return 0.5 * jnp.tanh(0.5 * v) + 0.5


def silu(v):
    half = 0.5 * v
    return half + half * jnp.tanh(half)


def record_kernel(node_ref, coords_ref, out_ref, parts_ref):
    parts_ref[...] = jnp.zeros_like(parts_ref)
    for a in range(3):
        value = coords_ref[a]
        high = value.astype(BF16).astype(F32)
        rest = value - high
        mid = rest.astype(BF16).astype(F32)
        parts_ref[pl.ds(PIECES + 3 * a, 3), :] = high
        parts_ref[pl.ds(PIECES + 16 + 3 * a, 3), :] = mid
        parts_ref[pl.ds(PIECES + 32 + 3 * a, 3), :] = rest - mid
    eye = (iota((GROUP, GROUP), 0) == iota((GROUP, GROUP), 1)).astype(F32).astype(BF16)
    widen = (iota((64, 128), 0) == iota((64, 128), 1)).astype(F32).astype(BF16)
    record = dot(node_ref[...], widen) + dot_nt(eye, parts_ref[...].astype(BF16))
    out_ref[...] = jnp.broadcast_to(record.astype(BF16)[None], out_ref.shape)


def records(node_state, coords, copies):
    return pl.pallas_call(
        record_kernel,
        out_shape=jax.ShapeDtypeStruct((copies, GROUP, 128), BF16),
        scratch_shapes=[pltpu.VMEM((128, GROUP), F32)],
        name="records",
    )(node_state, coords)


def vmem():
    return pl.BlockSpec(memory_space=pltpu.VMEM)


def in_hbm(v):
    return pltpu.with_memory_space_constraint(v, pltpu.HBM)


def hbm():
    return pl.BlockSpec(memory_space=pltpu.HBM)


def select_kernel(lists_hbm, pair_ref, found_ref, mark_ref, lists_ref, tile_ref, rank_ref, sems, lists_sem):
    groups = sems.shape[0]

    def fetch(g):
        rows = pl.ds(g * GROUP, GROUP)
        return pltpu.make_async_copy(pair_ref.at[rows], tile_ref.at[rows], sems.at[g])

    lists_copy = pltpu.make_async_copy(lists_hbm, lists_ref, lists_sem)
    lists_copy.start()
    start = lax.axis_index("col") * 128
    rows = groups * GROUP
    square = (128, 128)
    before = (iota(square, 0) < iota(square, 1)).astype(F32).astype(BF16)
    eye = (iota(square, 0) == iota(square, 1)).astype(F32).astype(BF16)
    one, other = iota((rows, rows), 0), iota((rows, rows), 1)
    earlier = (lax.shift_right_logical(one, 4) == lax.shift_right_logical(other, 4)) & (one > other)
    earlier = jnp.where(earlier, 1.0, 0.0).astype(BF16)
    lists_copy.wait()
    for g in range(groups):
        fetch(g).start()
    column = iota((128, rows), 0) + start
    chosen = jnp.zeros((128, rows), F32)
    for k in range(K):
        chosen = jnp.where(lists_ref[k : k + 1, :] == column, 1.0, chosen)
    chosen = chosen.astype(BF16)
    totals = dot_t(chosen, jnp.ones(square, BF16)).astype(BF16)
    rank = dot_t(chosen, before) + dot(earlier, totals)
    rank_ref[...] = jnp.where(dot_t(chosen, eye) > 0.0, rank, -1.0)
    slot = iota((SLOTS, 128), 0).astype(F32)

    def group(g, carry):
        fetch(g).wait()
        mark = jnp.zeros((SLOTS, 128), F32)
        picks = []
        ranks = rank_ref[pl.ds(pl.multiple_of(g * GROUP, GROUP), GROUP), :]
        for i in range(GROUP):
            hit = slot == ranks[i : i + 1, :]
            mark = jnp.where(hit, i + 1.0, mark)
            picks.append(jnp.where(hit, 1.0, 0.0).astype(BF16))
        pick = jnp.concatenate(picks, axis=1)
        spots = pl.ds(pl.multiple_of(g * SLOTS, SLOTS), SLOTS)
        tile = tile_ref[pl.ds(pl.multiple_of(g * GROUP, GROUP), GROUP)]
        found_ref[spots, :] = dot(pick, tile.reshape(GROUP * 128, 128)).astype(BF16)
        mark_ref[spots, :] = mark.astype(BF16)
        return carry

    lax.fori_loop(0, groups, group, 0, unroll=4)


def select_edges(lists, pair):
    groups = pair.shape[0] // GROUP
    return pl.pallas_call(
        select_kernel,
        in_specs=[hbm(), hbm()],
        out_specs=[vmem()] * 2,
        out_shape=[jax.ShapeDtypeStruct((groups * SLOTS, 128), BF16)] * 2,
        scratch_shapes=[
            pltpu.VMEM(lists.shape, jnp.int32),
            pltpu.VMEM(pair.shape, BF16),
            pltpu.VMEM((pair.shape[0], 128), F32),
            pltpu.SemaphoreType.DMA((groups,)),
            pltpu.SemaphoreType.DMA,
        ],
        compiler_params=pltpu.CompilerParams(vmem_limit_bytes=VMEM_LIMIT),
        cost_estimate=pl.CostEstimate(flops=3_000_000_000, bytes_accessed=9 * 2**20, transcendentals=0),
        name="select_edges",
    )(in_hbm(lists), in_hbm(pair))


def edge_kernel(
    found_ref,
    mark_ref,
    table_ref,
    w_edge_ref,
    w_radial_ref,
    w_query_ref,
    w_keyval_ref,
    w_edge_kv_ref,
    w_move_ref,
    out_ref,
    w_edge_s,
    w_keyval_s,
    w_query_s,
    w_radial_s,
    w_mix_s,
    w_move_s,
    rows_ref,
):
    col = lax.axis_index("col")
    for ref in (w_edge_s, w_keyval_s, w_query_s, w_radial_s, w_mix_s, w_move_s):
        ref[...] = jnp.zeros_like(ref)
    w_edge_s[0:64, :] = w_edge_ref[...]
    w_keyval_s[0:64, :] = w_keyval_ref[...]
    w_query_s[0:64, 0:64] = w_query_ref[...]
    w_radial_s[0:36, 0:64] = w_radial_ref[...]
    w_mix_s[0:64, :] = w_edge_kv_ref[...]
    w_move_s[0:12, 0:64] = w_move_ref[...]
    rows = table_ref[pl.ds(pl.multiple_of(lax.axis_index("row") * 256, 256), 256), :]
    rows_ref[...] = rows
    cols = table_ref[pl.ds(pl.multiple_of(col * 128, 128), 128), :]
    keyval = dot(cols, w_keyval_s[...]).astype(BF16)
    by_column = jnp.concatenate([keyval, cols], axis=1)
    lane = iota((1, 128), 1)
    source = iota((256, 256), 0)
    target = iota((256, 256), 1)
    channel = jnp.bitwise_and(source, 127)
    head = lax.shift_right_logical(channel, 4)
    for_value = (target >= 64) & (target < 128) & (lax.shift_right_logical(target - 64, 4) == head)
    for_move = (target >= 128) & (target < 140) & (jnp.bitwise_and(target, 3) == head)
    heads = jnp.where((channel < 64) & (for_value | for_move), 0.125, 0.0).astype(BF16)
    source = jnp.bitwise_and(iota((256, 128), 0), 127)
    target = iota((256, 128), 1) - PIECES
    low_atom = lax.shift_right_logical(source, 2) * 3
    spread = jnp.where(
        (source < 12) & (target >= low_atom) & (target < low_atom + 3), 1.0, 0.0
    ).astype(BF16)
    centre = lane.astype(F32) * CENTRE_STEP
    alpha = jnp.where((lane >= PIECES + 3) & (lane < PIECES + 6), 1.0, 0.0)
    per = GROUPS_PER_STEP * SLOTS
    own = GROUPS_PER_STEP * GROUP
    steps = found_ref.shape[0] // per
    shift_by = lax.shift_right_logical(iota((per, 128), 0), 7) * GROUP
    parts = []
    for step in range(steps):
        mark = mark_ref[pl.ds(step * per, per), :].astype(F32)
        residue = jnp.sum(mark, axis=1, keepdims=True) - 1.0
        pick_col = jnp.where(mark > 0.0, 1.0, 0.0).astype(BF16)
        target_row = jnp.where((lane >= shift_by) & (lane < shift_by + GROUP), lane - shift_by, -2).astype(F32)
        pick_row = jnp.where(residue == target_row, 1.0, 0.0).astype(BF16)
        rows = rows_ref[pl.ds(step * own, own), :]
        rows = jnp.concatenate([rows, jnp.zeros((128 - own, 128), BF16)], axis=0)
        from_col = dot(pick_col, by_column)
        from_row = dot(pick_row, rows)
        gap = from_col[:, 128:] - from_row
        relative = gap + pltpu.roll(gap, 112, 1) + pltpu.roll(gap, 96, 1)
        distance = jnp.sqrt(jnp.sum(relative * relative * alpha, axis=1, keepdims=True))
        offset = (distance - centre) * 2.0
        basis = jnp.exp(-(offset * offset)).astype(BF16)
        found = found_ref[pl.ds(step * per, per), :]
        hidden = silu(dot_nt(found, w_edge_s[...]) + dot(basis, w_radial_s[...])).astype(BF16)
        keyval_edge = from_col[:, :128] + dot(hidden, w_mix_s[...])
        queries = dot(from_row.astype(BF16), w_query_s[...])
        attention = 0.5 * jnp.tanh(dot(split2(queries * keyval_edge), heads)) + 0.5
        values = attention[:, :128] * keyval_edge
        moves = attention[:, 128:] * dot_nt(hidden, w_move_s[...])
        move = dot(split2(moves), spread) * relative
        both = jnp.where(lane < 64, pltpu.roll(move, 64, 1), values)
        summed = dot_t(pick_row, split2(both))
        parts.append((summed[:own, :128] + summed[:own, 128:]) * (1.0 / K))
    total = jnp.concatenate(parts, axis=0)
    atoms = rows_ref[...].astype(F32)
    atoms = atoms + pltpu.roll(atoms, 112, 1) + pltpu.roll(atoms, 96, 1)
    first = jnp.where(col == 0, 1.0, 0.0)
    total = total + jnp.where(lane < 9, pltpu.roll(atoms, 64, 1), 0.0) * first
    by_lane = jnp.transpose(total)
    groups = out_ref.shape[0]
    for d in range(groups):
        out_ref[d, 0:16, :] = total[d * GROUP : (d + 1) * GROUP, :]
        out_ref[d, 16:24, :] = by_lane[0:8, 0:128]
        out_ref[d, 24:32, :] = by_lane[0:8, 128:256]
        out_ref[d, 32:40, :] = jnp.concatenate(
            [by_lane[8:9, 0:128], by_lane[8:9, 128:256], jnp.zeros((6, 128), F32)], axis=0
        )


def edge_sums(found, mark, table, w_edge, w_radial, w_query, w_keyval, w_edge_kv, w_move):
    groups = found.shape[0] // SLOTS
    operands = (found, mark, table, w_edge, w_radial, w_query, w_keyval, w_edge_kv, w_move)
    whole = lambda shape: pl.BlockSpec(shape, lambda i: (0,) * len(shape))
    return pl.pallas_call(
        edge_kernel,
        grid=(1,),
        in_specs=[whole(a.shape) for a in operands],
        out_specs=whole((groups, 40, 128)),
        scratch_shapes=[pltpu.VMEM((128, 128), BF16)] * 6 + [pltpu.VMEM((groups * GROUP, 128), BF16)],
        out_shape=jax.ShapeDtypeStruct((groups, 40, 128), F32),
        compiler_params=pltpu.CompilerParams(vmem_limit_bytes=VMEM_LIMIT),
        cost_estimate=pl.CostEstimate(flops=2_000_000_000, bytes_accessed=3 * 2**20, transcendentals=0),
        name="edge_sums",
    )(*operands)


def total_kernel(parts_ref, node_ref, w_out_ref, node_out_ref, own_ref, rows_ref, send_ref, w_ref):
    col = lax.axis_index("col")
    total = parts_ref[0]
    for d in range(1, parts_ref.shape[0]):
        total = total + parts_ref[d]
    w_ref[...] = jnp.zeros_like(w_ref)
    w_ref[64:128, :] = w_out_ref[...]
    message = total[0:16, :].astype(BF16)
    node_out_ref[...] = node_ref[...].astype(F32) + dot(message, w_ref[...])
    left = jnp.concatenate([total[16:24, :], total[32:33, :], jnp.zeros((7, 128), F32)], axis=0)
    right = jnp.concatenate([total[24:32, :], total[33:34, :], jnp.zeros((7, 128), F32)], axis=0)
    rows_ref[:, 0:128] = left
    rows_ref[:, 128:256] = right
    odd = jnp.bitwise_and(col, 1) == 1
    send_ref[...] = jnp.broadcast_to(jnp.where(odd, right, left)[None], send_ref.shape)
    mine = jnp.where(col >= 8, right, left)
    mine = pltpu.roll(mine, jnp.bitwise_and(128 - jnp.bitwise_and(col, 7) * GROUP, 127), 1)
    for a in range(3):
        own_ref[a] = mine[3 * a : 3 * a + 3, 0:GROUP]


def totals(parts, node_state, w_out, copies):
    operands = (parts, node_state, w_out)
    shapes = ((GROUP, 64), (3, 3, GROUP), (16, 256), (copies, 16, 128))
    whole = lambda shape: pl.BlockSpec(shape, lambda i: (0,) * len(shape))
    return pl.pallas_call(
        total_kernel,
        grid=(1,),
        in_specs=[whole(a.shape) for a in operands],
        out_specs=[whole(shape) for shape in shapes],
        out_shape=[jax.ShapeDtypeStruct(shape, F32) for shape in shapes],
        scratch_shapes=[pltpu.VMEM((128, 64), BF16)],
        compiler_params=pltpu.CompilerParams(vmem_limit_bytes=SMALL_LIMIT),
        name="totals",
    )(*operands)


def transition_step(x, w_in, w_out, half_gate):
    x = x.astype(F32)
    centred = x - jnp.mean(x, axis=1, keepdims=True)
    mean = jnp.full((128, 128), 1.0 / 128.0, BF16)
    scale = lax.rsqrt(dot((centred * centred).astype(BF16), mean) + 1e-05)
    normed = (centred * scale).astype(BF16)
    hidden = jnp.maximum(dot(normed, w_in).astype(BF16), 0)
    return x + dot(hidden, w_out), jnp.tanh(dot(normed, half_gate)) + 1.0


def halved(ref):
    return (ref[...].astype(F32) * 0.5).astype(BF16)


def transition_kernel(
    first, pair_ref, w_in_ref, w_out_ref, w_gate_ref, base_ref, gate_ref, x_s, base_s, gate_s, sems, sem
):
    count = x_s.shape[0]

    def fetch(n):
        rows = pl.ds(n * BLOCK, BLOCK)
        return pltpu.make_async_copy(pair_ref.at[pl.ds(first + n * BLOCK, BLOCK)], x_s.at[rows], sems.at[n])

    for n in range(count // BLOCK):
        fetch(n).start()
    half_gate = halved(w_gate_ref)
    per = 8

    def step(n, carry):
        fetch(n).wait()
        for i in range(0, BLOCK, per):
            rows = pl.ds(n * BLOCK + i, per)
            x = x_s[rows].reshape(per * 128, 128)
            base, gate = transition_step(x, w_in_ref[...], w_out_ref[...], half_gate)
            base_s[rows] = base.astype(BF16).reshape(per, 128, 128)
            gate_s[rows] = gate.astype(BF16).reshape(per, 128, 128)
        rows = pl.ds(n * BLOCK, BLOCK)
        pltpu.make_async_copy(base_s.at[rows], base_ref.at[rows], sem).start()
        pltpu.make_async_copy(gate_s.at[rows], gate_ref.at[rows], sem).start()
        return carry

    lax.fori_loop(0, count // BLOCK, step, 0)
    pltpu.make_async_copy(base_s, base_ref, sem).wait()
    pltpu.make_async_copy(gate_s, gate_ref, sem).wait()


def transition(pair, w_in, w_out, w_gate, first, count):
    shape = (count,) + pair.shape[1:]
    return pl.pallas_call(
        functools.partial(transition_kernel, first),
        in_specs=[hbm()] + [vmem()] * 3,
        out_specs=[hbm()] * 2,
        out_shape=[pltpu.HBM(shape, BF16)] * 2,
        scratch_shapes=[pltpu.VMEM(shape, BF16)] * 3
        + [pltpu.SemaphoreType.DMA((count // BLOCK,)), pltpu.SemaphoreType.DMA],
        compiler_params=pltpu.CompilerParams(vmem_limit_bytes=VMEM_LIMIT),
        cost_estimate=pl.CostEstimate(
            flops=count * 128 * 2 * 128 * 640, bytes_accessed=count * 128 * 128 * 6, transcendentals=0
        ),
        name="transition",
    )(in_hbm(pair), w_in, w_out, w_gate)


def structure_kernel(
    counts, rows_ref, chain_ref, cols_ref, chains_ref, w_in_ref, w_out_ref, w_up_ref, w_down_ref, w_gate_ref, pair_ref, *refs
):
    held = refs[: 2 * len(counts)]
    out_ref, base_s, gate_s, made_s, w_in_s, w_out_s, sems, sem = refs[2 * len(counts) :]
    done = sum(counts)
    total = base_s.shape[0]
    blocks = total // BLOCK

    def fetch(n):
        at = n * BLOCK
        rows = pl.ds(at, BLOCK)
        if at >= done:
            return [pltpu.make_async_copy(pair_ref.at[rows], base_s.at[rows], sems.at[n])]
        part = 0
        while at >= counts[part]:
            at -= counts[part]
            part += 1
        source = pl.ds(at, BLOCK)
        return [
            pltpu.make_async_copy(held[2 * part].at[source], base_s.at[rows], sems.at[n]),
            pltpu.make_async_copy(held[2 * part + 1].at[source], gate_s.at[rows], sems.at[blocks + n]),
        ]

    for n in range(blocks):
        for copy in fetch(n):
            copy.start()
    row_index = lax.axis_index("row")
    col_index = lax.axis_index("col")
    w_in_s[...] = jnp.zeros_like(w_in_s)
    w_out_s[...] = jnp.zeros_like(w_out_s)
    half = halved(w_in_ref)
    for k in range(2):
        w_in_s[48 * k : 48 * k + 36, 128 * k : 128 * (k + 1)] = half[0:36]
        w_in_s[48 * k + 40 : 48 * k + 46, 128 * k : 128 * (k + 1)] = half[36:42]
        w_out_s[128 * k : 128 * (k + 1), 128 * k : 128 * (k + 1)] = halved(w_out_ref)
    half_gate = halved(w_gate_ref)

    cols = cols_ref[lax.shift_right_logical(col_index, 1)]
    wide = lambda v: jnp.broadcast_to(v, (8, 128))
    alpha = [wide(cols[3 + x : 4 + x, :]) for x in range(3)]
    feature = iota((8, 128), 0)
    bonds = [
        jnp.where(
            feature == 2,
            alpha[x] - wide(cols[x : x + 1, :]),
            jnp.where(feature == 3, alpha[x] - wide(cols[6 + x : 7 + x, :]), 0.0),
        )
        for x in range(3)
    ]
    chain = wide(chains_ref[pl.ds(col_index, 1), :])
    position = iota((8, 128), 1) + col_index * 128
    centre = [(iota((8, 128), 0) + 8 * b).astype(F32) * CENTRE_STEP for b in range(5)]

    def features(row):
        p = [rows_ref[3 + x, row] for x in range(3)]
        rn = [rows_ref[x, row] - p[x] for x in range(3)]
        rc = [rows_ref[6 + x, row] - p[x] for x in range(3)]
        gap = [alpha[x] - p[x] for x in range(3)]
        square = gap[0] * gap[0] + gap[1] * gap[1] + gap[2] * gap[2]
        distance = jnp.sqrt(square)
        inverse = 1.0 / (1.0 + distance)
        vectors = [
            jnp.where(feature == 0, rn[x], jnp.where(feature == 1, rc[x], bonds[x])) for x in range(3)
        ]
        orient = (vectors[0] * gap[0] + vectors[1] * gap[1] + vectors[2] * gap[2]) * inverse
        at = row + row_index * 256
        same = jnp.where(chain == chain_ref[at], 1.0, 0.0)
        offset = same * (jnp.clip(position - at, -32, 32).astype(F32) * (1.0 / 32.0))
        tail = jnp.where(feature == 4, same, jnp.where(feature == 5, offset, orient))
        tail = jnp.where(feature < 6, tail, 0.0)
        basis = []
        for b in range(5):
            t = (distance - centre[b]) * 2.0
            basis.append(jnp.exp(-(t * t)))
        return basis + [tail]

    per = 16

    def terms(start):
        feats = []
        for u in range(per // 2):
            row = start + 2 * u
            feats.append(jnp.concatenate(features(row) + features(row + 1), axis=0).astype(BF16))
        half = dot_t(jnp.concatenate(feats, axis=1), w_in_s[...])
        hidden = (half + half * jnp.tanh(half)).astype(BF16)
        term = dot(hidden, w_out_s[...])
        return [
            term[128 * (u // 2) : 128 * (u // 2 + 1), 128 * (u % 2) : 128 * (u % 2 + 1)] for u in range(per)
        ]

    def finish_held(start):
        for u, term in enumerate(terms(start)):
            gate = gate_s[start + u].astype(F32)
            made_s[start + u] = (base_s[start + u].astype(F32) + gate * term).astype(BF16)

    def finish_whole(start):
        term = terms(start)
        for i in range(0, per, 8):
            x = base_s[pl.ds(start + i, 8)].reshape(8 * 128, 128)
            base, gate = transition_step(x, w_up_ref[...], w_down_ref[...], half_gate)
            for u in range(8):
                spot = slice(128 * u, 128 * (u + 1))
                made_s[start + i + u] = (base[spot] + gate[spot] * term[i + u]).astype(BF16)

    def send(n):
        rows = pl.ds(n * BLOCK, BLOCK)
        pltpu.make_async_copy(made_s.at[rows], out_ref.at[rows], sem).start()

    def await_block(n, pair_too):
        rows = pl.ds(n * BLOCK, BLOCK)
        pltpu.make_async_copy(pair_ref.at[rows], base_s.at[rows], sems.at[n]).wait()
        if pair_too:
            pltpu.make_async_copy(pair_ref.at[rows], gate_s.at[rows], sems.at[blocks + n]).wait()

    def step(finish, pair_too, n, carry):
        await_block(n, pair_too)
        for i in range(0, BLOCK, per):
            finish(n * BLOCK + i)
        send(n)
        return carry

    lax.fori_loop(0, done // BLOCK, functools.partial(step, finish_held, True), 0)
    lax.fori_loop(done // BLOCK, blocks, functools.partial(step, finish_whole, False), 0)
    pltpu.make_async_copy(made_s, out_ref, sem).wait()


def structure(rows, chain, cols, w_in, w_out, w_up, w_down, w_gate, pair, held):
    smem = pl.BlockSpec(memory_space=pltpu.SMEM)
    counts = tuple(base.shape[0] for base in held[0::2])
    blocks = pair.shape[0] // BLOCK
    return pl.pallas_call(
        functools.partial(structure_kernel, counts),
        in_specs=[smem, smem] + [vmem()] * 7 + [hbm()] * (1 + len(held)),
        out_specs=hbm(),
        scratch_shapes=[pltpu.VMEM(pair.shape, BF16)] * 3
        + [
            pltpu.VMEM((96, 256), BF16),
            pltpu.VMEM((256, 256), BF16),
            pltpu.SemaphoreType.DMA((2 * blocks,)),
            pltpu.SemaphoreType.DMA,
        ],
        out_shape=jax.ShapeDtypeStruct(pair.shape, BF16),
        compiler_params=pltpu.CompilerParams(vmem_limit_bytes=VMEM_LIMIT),
        name="structure",
    )(rows, chain, cols, chain.reshape(-1, 128), w_in, w_out, w_up, w_down, w_gate, in_hbm(pair), *map(in_hbm, held))


def exchange(v, axis):
    return lax.all_to_all(v, axis, split_axis=0, concat_axis=0, tiled=True)


def local(
    pair,
    node_state,
    coords,
    neighbours,
    chain,
    w_edge,
    w_radial,
    w_query,
    w_keyval,
    w_edge_kv,
    w_out,
    w_move,
    w_trans_in,
    w_trans_out,
    w_gate,
    w_feat_in,
    w_feat_out,
):
    row_devices = lax.axis_size("row")
    col_devices = lax.axis_size("col")
    step = functools.partial(transition, w_in=w_trans_in, w_out=w_trans_out, w_gate=w_gate)

    table = exchange(records(node_state, coords, row_devices * col_devices), BOTH)
    found, mark = select_edges(neighbours.T, pair)
    parts = edge_sums(
        found,
        mark,
        table.reshape(-1, 128),
        w_edge.T,
        w_radial,
        w_query,
        w_keyval,
        w_edge_kv,
        w_move.T,
    )
    pair, parts = lax.optimization_barrier((pair, parts))
    parts = exchange(parts, "col")
    held = step(pair, first=0, count=FIRST)
    node_out, own, rows, send = totals(parts, node_state, w_out, row_devices)
    pair, send = lax.optimization_barrier((pair, send))
    cols = exchange(send, "row")
    held += step(pair, first=FIRST, count=SECOND)
    pair_out = structure(
        rows, chain, cols, w_feat_in, w_feat_out, w_trans_in, w_trans_out, w_gate, pair, held
    )
    return (pair_out, node_out, own)


def solution(mesh):
    spread = P(None, None, BOTH)
    in_specs = (P("row", "col", None), P(BOTH, None), spread, P("row", None)) + (P(),) * 13
    out_specs = (P("row", "col", None), P(BOTH, None), spread)
    return jax.shard_map(local, mesh=mesh, in_specs=in_specs, out_specs=out_specs, check_vma=False)
```

time: 110 us -> 79 us (0.72)
  Pallas kernels: 76.9 us -> 51.6 us
  local copies, waits for them, and re-layouts: 7.28 us -> 0.08 us
  waiting for transfers between devices: 0.01 us -> 6.21 us
  starting transfers between devices: 23.6 us -> 19.6 us
    pallas_call x7 -> x6, Pallas kernels: 75.2 us -> 49.9 us  [the longest x1 17.9 us: structure(): pl.pallas_call(functools.partial(structure_kernel, counts), in_specs=[sme...]
    all_to_all x3, waiting for transfers between devices: 0.01 us -> 6.21 us  [exchange(): return lax.all_to_all(v, axis, split_axis=0, concat_axis=0, tiled=True)]
    unnamed x35 -> x28, local copies, waits for them, and re-layouts: 5.76 us -> 0.08 us
    all_to_all x3, starting transfers between devices: 23.6 us -> 19.6 us  [exchange(): return lax.all_to_all(v, axis, split_axis=0, concat_axis=0, tiled=True)]
  transfers between devices with their start and end apart: 3 -> 3, of which waited for: 0 -> 1; matrix products, arithmetic and copies ran while one was open for 4% -> 0% of each run, Pallas kernels for 44% -> 30%
where the time goes in v2:
time: 79 us; the launch traced here: 78.5 us
  Pallas kernels  51.6 us (65%)
  starting transfers between devices  19.6 us (25%)
  waiting for transfers between devices  6.21 us (8%)
  between operations  1.03 us (1%)
    all_to_all x3, starting transfers between devices, exchange(): return lax.all_to_all(v, axis, split_axis=0, concat_axis=0, tiled=True)  19.6 us
    pallas_call x1, Pallas kernels, structure(): pl.pallas_call(functools.partial(structure_kernel, counts), in_specs=[sme...  17.9 us
    pallas_call x2, Pallas kernels, transition(): pl.pallas_call(functools.partial(transition_kernel, first), in_specs=[hbm...  16.7 us
    pallas_call x1, Pallas kernels, edge_sums(): pl.pallas_call(edge_kernel, grid=(1,), in_specs=[whole(a.shape) for a in...  7.49 us
    pallas_call x1, Pallas kernels, select_edges(): pl.pallas_call(select_kernel, in_specs=[hbm(), hbm()], out_specs=[vmem()]...  7.05 us
    all_to_all x3, waiting for transfers between devices, exchange(): return lax.all_to_all(v, axis, split_axis=0, concat_axis=0, tiled=True)  6.21 us
    pallas_call x1, Pallas kernels, records(): pl.pallas_call(record_kernel, out_shape=jax.ShapeDtypeStruct((copies, GRO...  1.7 us
  transfers between devices with their start and end apart: 3, of which 1 were waited for; matrix products, arithmetic and copies ran while one was open for 0% of the time, Pallas kernels for 30%

profile of v2, /device:TPU:1, one launch (start us, length us, event | category | flops | bytes accessed | tf_op | source)
XLA Modules:
  0.0 78.5 jit_solution(13675048864896270617)
XLA Ops:
  0.6 1.7 %records.1 = bf16[128,16,128]{2,1,0:T(8,128)(2,1)} custom-call(bf16[16,64]{1,0:T(8,128)(2,1)} %node_ref.3, f32[3,3,16]{2,1,0:T(4,128)} %coords_ref.1), custom_call_target="tpu_custom_call" | custom-call | tf_op jit(solution)/shard_map/records/pallas_call | solution.py:75
  2.3 11.5 %all-to-all-start = ((bf16[128,16,128]{2,1,0:T(8,128)(2,1)}), bf16[128,16,128]{2,1,0:T(8,128)(2,1)S(1)}, u32[]{:S(2)}, u32[]{:S(2)}) async-start(bf16[128,16,128]{2,1,0:T(8,128)(2,1)} %records.1), calls=%async_computation | async-start | bytes 1048576 | tf_op jit(solution)/shard_map/all_to_all | solution.py:526
  13.8 0.0 copy-start.8
  13.8 0.0 copy-start.9
  13.9 0.0 copy-start.10
  13.9 0.0 copy-start.11
  13.9 0.0 copy-start.12
  13.9 0.0 copy-start.13
  13.9 7.0 %select_edges.1 = (bf16[2048,128]{1,0:T(8,128)(2,1)S(1)}, bf16[2048,128]{1,0:T(8,128)(2,1)S(1)}) custom-call(s32[64,256]{1,0:T(8,128)} %bitcast.9, bf16[256,128,128]{2,1,0:T(8,128)(2,1)} %pair_ref.4), custom_call_target="tpu_custom_call" | custom-call | flops 3000000000 | bytes 9437184 | tf_op jit(solution)/shard_map/select_edges/pallas_call | solution.py:146
  21.0 6.2 %all-to-all-done = bf16[128,16,128]{2,1,0:T(8,128)(2,1)S(1)} async-done(((bf16[128,16,128]{2,1,0:T(8,128)(2,1)}), bf16[128,16,128]{2,1,0:T(8,128)(2,1)S(1)}, u32[]{:S(2)}, u32[]{:S(2)}) %all-to-all-start) | async-done | bytes 524320 | tf_op jit(solution)/shard_map/all_to_all | solution.py:526
  27.2 0.0 copy-done.8
  27.2 0.0 copy-done.9
  27.2 0.0 copy-done.10
  27.2 0.0 copy-done.11
  27.2 0.0 copy-done.12
  27.2 0.0 copy-done.13
  27.2 0.0 copy-start
  27.2 0.0 copy-start.1
  27.2 0.0 copy-start.2
  27.2 7.5 %edge_sums.1 = f32[16,40,128]{2,1,0:T(8,128)} custom-call(bf16[2048,128]{1,0:T(8,128)(2,1)S(1)} %get-tuple-element.17.found_ref, bf16[2048,128]{1,0:T(8,128)(2,1)S(1)} %get-tuple-element.18.mark_ref, bf16[2048,128]{1,0:T(8,128)(2,1)S(1)} %bitcast.5, bf16[64,128]{1,0:T(8,128)(2,1)S(1)} %bitcast.7, bf16[36,64]{1,0:T(8,128)(2,1)S(1)} %copy-done.12, ...), custom_call_target="tpu_custom_call" | custom-call | flops 2000000000 | bytes 3145728 | tf_op jit(solution)/shard_map/edge_sums/pallas_call | solution.py:264
  34.7 3.5 %all-to-all-start.1 = ((f32[16,40,128]{2,1,0:T(8,128)}), f32[16,40,128]{2,1,0:T(8,128)S(1)}, u32[]{:S(2)}, u32[]{:S(2)}) async-start(f32[16,40,128]{2,1,0:T(8,128)} %edge_sums.1), calls=%async_computation.1 | async-start | bytes 655360 | tf_op jit(solution)/shard_map/all_to_all | solution.py:526
  38.3 0.0 copy-done
  38.3 0.0 copy-done.1
  38.3 0.0 copy-done.2
  38.3 0.0 copy-start.5
  38.3 0.0 copy-start.6
  38.3 9.5 %transition.2 = (bf16[96,128,128]{2,1,0:T(8,128)(2,1)}, bf16[96,128,128]{2,1,0:T(8,128)(2,1)}) custom-call(bf16[256,128,128]{2,1,0:T(8,128)(2,1)} %pair_ref.4, bf16[128,256]{1,0:T(8,128)(2,1)S(1)} %copy-done, bf16[256,128]{1,0:T(8,128)(2,1)S(1)} %copy-done.1, bf16[128,128]{1,0:T(8,128)(2,1)S(1)} %copy-done.2), custom_call_target="tpu_custom_call" | custom-call | flops 2013265920 | bytes 9437184 | tf_op jit(solution)/shard_map/transition/pallas_call | solution.py:362
  47.8 0.0 all-to-all-done.1.parts_ref
  47.8 0.0 copy-done.5
  47.8 0.0 copy-done.6
  47.9 0.7 totals.1
  48.6 4.6 %all-to-all-start.2 = ((f32[8,16,128]{2,1,0:T(8,128)}), f32[8,16,128]{2,1,0:T(8,128)S(1)}, u32[]{:S(2)}, u32[]{:S(2)}) async-start(f32[8,16,128]{2,1,0:T(8,128)} %get-tuple-element.23), calls=%async_computation.2 | async-start | bytes 131072 | tf_op jit(solution)/shard_map/all_to_all | solution.py:526
  53.2 0.0 copy-start.3
  53.2 0.0 copy-start.4
  53.2 0.0 copy-start.7
  53.2 7.2 %transition.3 = (bf16[64,128,128]{2,1,0:T(8,128)(2,1)}, bf16[64,128,128]{2,1,0:T(8,128)(2,1)}) custom-call(bf16[256,128,128]{2,1,0:T(8,128)(2,1)} %pair_ref.4, bf16[128,256]{1,0:T(8,128)(2,1)S(1)} %copy-done, bf16[256,128]{1,0:T(8,128)(2,1)S(1)} %copy-done.1, bf16[128,128]{1,0:T(8,128)(2,1)S(1)} %copy-done.2), custom_call_target="tpu_custom_call" | custom-call | flops 1342177280 | bytes 6291456 | tf_op jit(solution)/shard_map/transition/pallas_call | solution.py:362
  60.4 0.0 all-to-all-done.2.cols_ref
  60.4 0.0 copy-done.3
  60.4 0.0 copy-done.4
  60.5 0.0 copy-done.7
  60.5 17.9 %structure.1 = bf16[256,128,128]{2,1,0:T(8,128)(2,1)} custom-call(f32[16,256]{1,0:T(8,128)S(1)} %get-tuple-element.20.rows_ref, s32[2048]{0:T(1024)S(1)} %copy-done.4, f32[8,16,128]{2,1,0:T(8,128)S(1)} %all-to-all-done.2.cols_ref, s32[16,128]{1,0:T(8,128)S(1)} %bitcast.6, bf16[42,128]{1,0:T(8,128)(2,1)S(1)} %copy-done.7, bf16[128,128]{1,0:T(8,128)(2,1)S(1)} %copy-done.3, ...), custom_call_target="tpu_custom_call" | custom-call | tf_op jit(solution)/shard_map/structure/pallas_call | solution.py:508
Async XLA Ops:
  2.3 24.8 %all-to-all-start = ((bf16[128,16,128]{2,1,0:T(8,128)(2,1)}), bf16[128,16,128]{2,1,0:T(8,128)(2,1)S(1)}, u32[]{:S(2)}, u32[]{:S(2)}) async-start(bf16[128,16,128]{2,1,0:T(8,128)(2,1)} %records.1), calls=%async_computation | async-start | bytes 1048576 | tf_op jit(solution)/shard_map/all_to_all | solution.py:526
  13.8 13.3 %copy-start.8 = (bf16[128,64]{0,1:T(8,128)(2,1)S(1)}, bf16[128,64]{0,1:T(8,128)(2,1)}, u32[]{:S(2)}) copy-start(bf16[128,64]{0,1:T(8,128)(2,1)} %param.22) | copy-start | bytes 49156
  13.8 13.3 %copy-start.9 = (bf16[64,64]{1,0:T(8,128)(2,1)S(1)}, bf16[64,64]{1,0:T(8,128)(2,1)}, u32[]{:S(2)}) copy-start(bf16[64,64]{1,0:T(8,128)(2,1)} %w_query_ref.1) | copy-start | bytes 24580
  13.9 13.3 %copy-start.10 = (bf16[64,128]{1,0:T(8,128)(2,1)S(1)}, bf16[64,128]{1,0:T(8,128)(2,1)}, u32[]{:S(2)}) copy-start(bf16[64,128]{1,0:T(8,128)(2,1)} %w_keyval_ref.1) | copy-start | bytes 49156
  13.9 13.3 %copy-start.11 = (bf16[64,128]{1,0:T(8,128)(2,1)S(1)}, bf16[64,128]{1,0:T(8,128)(2,1)}, u32[]{:S(2)}) copy-start(bf16[64,128]{1,0:T(8,128)(2,1)} %w_edge_kv_ref.1) | copy-start | bytes 49156
  13.9 13.3 %copy-start.12 = (bf16[36,64]{1,0:T(8,128)(2,1)S(1)}, bf16[36,64]{1,0:T(8,128)(2,1)}, u32[]{:S(2)}) copy-start(bf16[36,64]{1,0:T(8,128)(2,1)} %w_radial_ref.1) | copy-start | bytes 13828
  13.9 13.3 %copy-start.13 = (bf16[64,12]{0,1:T(8,128)(2,1)S(1)}, bf16[64,12]{0,1:T(8,128)(2,1)}, u32[]{:S(2)}) copy-start(bf16[64,12]{0,1:T(8,128)(2,1)} %param.28) | copy-start | bytes 4612
  27.2 11.1 %copy-start = (bf16[128,256]{1,0:T(8,128)(2,1)S(1)}, bf16[128,256]{1,0:T(8,128)(2,1)}, u32[]{:S(2)}) copy-start(bf16[128,256]{1,0:T(8,128)(2,1)} %w_up_ref.1) | copy-start | bytes 196612
  27.2 11.1 %copy-start.1 = (bf16[256,128]{1,0:T(8,128)(2,1)S(1)}, bf16[256,128]{1,0:T(8,128)(2,1)}, u32[]{:S(2)}) copy-start(bf16[256,128]{1,0:T(8,128)(2,1)} %w_down_ref.1) | copy-start | bytes 196612
  27.2 11.1 %copy-start.2 = (bf16[128,128]{1,0:T(8,128)(2,1)S(1)}, bf16[128,128]{1,0:T(8,128)(2,1)}, u32[]{:S(2)}) copy-start(bf16[128,128]{1,0:T(8,128)(2,1)} %w_gate_ref.5) | copy-start | bytes 98308
  34.7 13.1 %all-to-all-start.1 = ((f32[16,40,128]{2,1,0:T(8,128)}), f32[16,40,128]{2,1,0:T(8,128)S(1)}, u32[]{:S(2)}, u32[]{:S(2)}) async-start(f32[16,40,128]{2,1,0:T(8,128)} %edge_sums.1), calls=%async_computation.1 | async-start | bytes 655360 | tf_op jit(solution)/shard_map/all_to_all | solution.py:526
  38.3 9.5 %copy-start.5 = (bf16[16,64]{1,0:T(8,128)(2,1)S(1)}, bf16[16,64]{1,0:T(8,128)(2,1)}, u32[]{:S(2)}) copy-start(bf16[16,64]{1,0:T(8,128)(2,1)} %node_ref.3) | copy-start | bytes 6148
  38.3 9.5 %copy-start.6 = (bf16[64,64]{1,0:T(8,128)(2,1)S(1)}, bf16[64,64]{1,0:T(8,128)(2,1)}, u32[]{:S(2)}) copy-start(bf16[64,64]{1,0:T(8,128)(2,1)} %w_out_ref.4) | copy-start | bytes 24580
  48.6 11.8 %all-to-all-start.2 = ((f32[8,16,128]{2,1,0:T(8,128)}), f32[8,16,128]{2,1,0:T(8,128)S(1)}, u32[]{:S(2)}, u32[]{:S(2)}) async-start(f32[8,16,128]{2,1,0:T(8,128)} %get-tuple-element.23), calls=%async_computation.2 | async-start | bytes 131072 | tf_op jit(solution)/shard_map/all_to_all | solution.py:526
  53.2 7.2 %copy-start.3 = (bf16[128,128]{1,0:T(8,128)(2,1)S(1)}, bf16[128,128]{1,0:T(8,128)(2,1)}, u32[]{:S(2)}) copy-start(bf16[128,128]{1,0:T(8,128)(2,1)} %w_out_ref.7) | copy-start | bytes 98308
  53.2 7.3 %copy-start.4 = (s32[2048]{0:T(1024)S(1)}, s32[2048]{0:T(1024)}, u32[]{:S(2)}) copy-start(s32[2048]{0:T(1024)} %chain_ref.1) | copy-start | bytes 24580
  53.2 7.3 %copy-start.7 = (bf16[42,128]{1,0:T(8,128)(2,1)S(1)}, bf16[42,128]{1,0:T(8,128)(2,1)}, u32[]{:S(2)}) copy-start(bf16[42,128]{1,0:T(8,128)(2,1)} %w_in_ref.5) | copy-start | bytes 32260

commit v3 on v2

--- a/solution.py
+++ b/solution.py
@@ -16,12 +16,13 @@
 PIECES = 64
 GROUP = 16
 SLOTS = 128
-GROUPS_PER_STEP = 4
+GROUPS_PER_STEP = 8
 VMEM_LIMIT = 48 * 1024 * 1024
 SMALL_LIMIT = 8 * 1024 * 1024
 BLOCK = 32
-FIRST = 96
-SECOND = 64
+STEP = 8
+HELD_STEP = 16
+PARTS = (0, 96, 32)
 
 
 def iota(shape, dim):
@@ -92,7 +93,22 @@
     return pl.BlockSpec(memory_space=pltpu.HBM)
 
 
-def select_kernel(lists_hbm, pair_ref, found_ref, mark_ref, lists_ref, tile_ref, rank_ref, sems, lists_sem):
+def select_kernel(
+    lists_hbm,
+    pair_ref,
+    w_edge_hbm,
+    edge_ref,
+    pick_col_ref,
+    pick_row_ref,
+    lists_ref,
+    tile_ref,
+    rank_ref,
+    w_edge_ref,
+    w_edge_s,
+    sems,
+    lists_sem,
+    w_edge_sem,
+):
     groups = sems.shape[0]
 
     def fetch(g):
@@ -101,6 +117,8 @@
 
     lists_copy = pltpu.make_async_copy(lists_hbm, lists_ref, lists_sem)
     lists_copy.start()
+    w_edge_copy = pltpu.make_async_copy(w_edge_hbm, w_edge_ref, w_edge_sem)
+    w_edge_copy.start()
     start = lax.axis_index("col") * 128
     rows = groups * GROUP
     square = (128, 128)
@@ -121,6 +139,10 @@
     rank = dot_t(chosen, before) + dot(earlier, totals)
     rank_ref[...] = jnp.where(dot_t(chosen, eye) > 0.0, rank, -1.0)
     slot = iota((SLOTS, 128), 0).astype(F32)
+    lane = iota((1, 128), 1)
+    w_edge_copy.wait()
+    w_edge_s[...] = jnp.zeros_like(w_edge_s)
+    w_edge_s[0:64, :] = w_edge_ref[...]
 
     def group(g, carry):
         fetch(g).wait()
@@ -134,45 +156,53 @@
         pick = jnp.concatenate(picks, axis=1)
         spots = pl.ds(pl.multiple_of(g * SLOTS, SLOTS), SLOTS)
         tile = tile_ref[pl.ds(pl.multiple_of(g * GROUP, GROUP), GROUP)]
-        found_ref[spots, :] = dot(pick, tile.reshape(GROUP * 128, 128)).astype(BF16)
-        mark_ref[spots, :] = mark.astype(BF16)
+        found = dot(pick, tile.reshape(GROUP * 128, 128)).astype(BF16)
+        edge_ref[spots, :] = dot_nt(found, w_edge_s[...])
+        pick_col_ref[spots, :] = jnp.where(mark > 0.0, 1.0, 0.0).astype(BF16)
+        own = lane - lax.rem(g, GROUPS_PER_STEP) * GROUP
+        own = jnp.where((own >= 0) & (own < GROUP), own + 1, -1).astype(F32)
+        residue = jnp.sum(mark, axis=1, keepdims=True)
+        pick_row_ref[spots, :] = jnp.where(residue == own, 1.0, 0.0).astype(BF16)
         return carry
 
     lax.fori_loop(0, groups, group, 0, unroll=4)
 
 
-def select_edges(lists, pair):
+def select_edges(lists, pair, w_edge):
     groups = pair.shape[0] // GROUP
+    shape = (groups * SLOTS, 128)
     return pl.pallas_call(
         select_kernel,
-        in_specs=[hbm(), hbm()],
-        out_specs=[vmem()] * 2,
-        out_shape=[jax.ShapeDtypeStruct((groups * SLOTS, 128), BF16)] * 2,
+        in_specs=[hbm(), hbm(), hbm()],
+        out_specs=[vmem()] * 3,
+        out_shape=[jax.ShapeDtypeStruct(shape, dtype) for dtype in (F32, BF16, BF16)],
         scratch_shapes=[
             pltpu.VMEM(lists.shape, jnp.int32),
             pltpu.VMEM(pair.shape, BF16),
             pltpu.VMEM((pair.shape[0], 128), F32),
+            pltpu.VMEM(w_edge.shape, BF16),
+            pltpu.VMEM((128, 128), BF16),
             pltpu.SemaphoreType.DMA((groups,)),
+            pltpu.SemaphoreType.DMA,
             pltpu.SemaphoreType.DMA,
         ],
         compiler_params=pltpu.CompilerParams(vmem_limit_bytes=VMEM_LIMIT),
         cost_estimate=pl.CostEstimate(flops=3_000_000_000, bytes_accessed=9 * 2**20, transcendentals=0),
         name="select_edges",
-    )(in_hbm(lists), in_hbm(pair))
+    )(in_hbm(lists), in_hbm(pair), in_hbm(w_edge))
 
 
 def edge_kernel(
-    found_ref,
-    mark_ref,
+    edge_ref,
+    pick_col_ref,
+    pick_row_ref,
     table_ref,
-    w_edge_ref,
     w_radial_ref,
     w_query_ref,
     w_keyval_ref,
     w_edge_kv_ref,
     w_move_ref,
     out_ref,
-    w_edge_s,
     w_keyval_s,
     w_query_s,
     w_radial_s,
@@ -181,9 +211,8 @@
     rows_ref,
 ):
     col = lax.axis_index("col")
-    for ref in (w_edge_s, w_keyval_s, w_query_s, w_radial_s, w_mix_s, w_move_s):
+    for ref in (w_keyval_s, w_query_s, w_radial_s, w_mix_s, w_move_s):
         ref[...] = jnp.zeros_like(ref)
-    w_edge_s[0:64, :] = w_edge_ref[...]
     w_keyval_s[0:64, :] = w_keyval_ref[...]
     w_query_s[0:64, 0:64] = w_query_ref[...]
     w_radial_s[0:36, 0:64] = w_radial_ref[...]
@@ -212,17 +241,13 @@
     alpha = jnp.where((lane >= PIECES + 3) & (lane < PIECES + 6), 1.0, 0.0)
     per = GROUPS_PER_STEP * SLOTS
     own = GROUPS_PER_STEP * GROUP
-    steps = found_ref.shape[0] // per
-    shift_by = lax.shift_right_logical(iota((per, 128), 0), 7) * GROUP
+    steps = edge_ref.shape[0] // per
     parts = []
     for step in range(steps):
-        mark = mark_ref[pl.ds(step * per, per), :].astype(F32)
-        residue = jnp.sum(mark, axis=1, keepdims=True) - 1.0
-        pick_col = jnp.where(mark > 0.0, 1.0, 0.0).astype(BF16)
-        target_row = jnp.where((lane >= shift_by) & (lane < shift_by + GROUP), lane - shift_by, -2).astype(F32)
-        pick_row = jnp.where(residue == target_row, 1.0, 0.0).astype(BF16)
+        spots = pl.ds(step * per, per)
+        pick_col = pick_col_ref[spots, :]
+        pick_row = pick_row_ref[spots, :]
         rows = rows_ref[pl.ds(step * own, own), :]
-        rows = jnp.concatenate([rows, jnp.zeros((128 - own, 128), BF16)], axis=0)
         from_col = dot(pick_col, by_column)
         from_row = dot(pick_row, rows)
         gap = from_col[:, 128:] - from_row
@@ -230,8 +255,7 @@
         distance = jnp.sqrt(jnp.sum(relative * relative * alpha, axis=1, keepdims=True))
         offset = (distance - centre) * 2.0
         basis = jnp.exp(-(offset * offset)).astype(BF16)
-        found = found_ref[pl.ds(step * per, per), :]
-        hidden = silu(dot_nt(found, w_edge_s[...]) + dot(basis, w_radial_s[...])).astype(BF16)
+        hidden = silu(edge_ref[spots, :] + dot(basis, w_radial_s[...])).astype(BF16)
         keyval_edge = from_col[:, :128] + dot(hidden, w_mix_s[...])
         queries = dot(from_row.astype(BF16), w_query_s[...])
         attention = 0.5 * jnp.tanh(dot(split2(queries * keyval_edge), heads)) + 0.5
@@ -257,16 +281,16 @@
         )
 
 
-def edge_sums(found, mark, table, w_edge, w_radial, w_query, w_keyval, w_edge_kv, w_move):
-    groups = found.shape[0] // SLOTS
-    operands = (found, mark, table, w_edge, w_radial, w_query, w_keyval, w_edge_kv, w_move)
+def edge_sums(edge, pick_col, pick_row, table, w_radial, w_query, w_keyval, w_edge_kv, w_move):
+    groups = edge.shape[0] // SLOTS
+    operands = (edge, pick_col, pick_row, table, w_radial, w_query, w_keyval, w_edge_kv, w_move)
     whole = lambda shape: pl.BlockSpec(shape, lambda i: (0,) * len(shape))
     return pl.pallas_call(
         edge_kernel,
         grid=(1,),
-        in_specs=[whole(a.shape) for a in operands],
+        in_specs=[vmem()] * 4 + [whole(a.shape) for a in operands[4:]],
         out_specs=whole((groups, 40, 128)),
-        scratch_shapes=[pltpu.VMEM((128, 128), BF16)] * 6 + [pltpu.VMEM((groups * GROUP, 128), BF16)],
+        scratch_shapes=[pltpu.VMEM((128, 128), BF16)] * 5 + [pltpu.VMEM((groups * GROUP, 128), BF16)],
         out_shape=jax.ShapeDtypeStruct((groups, 40, 128), F32),
         compiler_params=pltpu.CompilerParams(vmem_limit_bytes=VMEM_LIMIT),
         cost_estimate=pl.CostEstimate(flops=2_000_000_000, bytes_accessed=3 * 2**20, transcendentals=0),
@@ -325,9 +349,9 @@
     return (ref[...].astype(F32) * 0.5).astype(BF16)
 
 
-def transition_kernel(
-    first, pair_ref, w_in_ref, w_out_ref, w_gate_ref, base_ref, gate_ref, x_s, base_s, gate_s, sems, sem
-):
+def transition_kernel(first, pair_ref, w_in_ref, w_out_ref, w_gate_ref, base_ref, gate_ref, x_s, *refs):
+    base_s, gate_s = refs[:2] if len(refs) == 4 else (base_ref, gate_ref)
+    sems, sem = refs[-2:]
     count = x_s.shape[0]
 
     def fetch(n):
@@ -337,34 +361,35 @@
     for n in range(count // BLOCK):
         fetch(n).start()
     half_gate = halved(w_gate_ref)
-    per = 8
 
     def step(n, carry):
         fetch(n).wait()
-        for i in range(0, BLOCK, per):
-            rows = pl.ds(n * BLOCK + i, per)
-            x = x_s[rows].reshape(per * 128, 128)
+        for i in range(0, BLOCK, STEP):
+            rows = pl.ds(n * BLOCK + i, STEP)
+            x = x_s[rows].reshape(STEP * 128, 128)
             base, gate = transition_step(x, w_in_ref[...], w_out_ref[...], half_gate)
-            base_s[rows] = base.astype(BF16).reshape(per, 128, 128)
-            gate_s[rows] = gate.astype(BF16).reshape(per, 128, 128)
-        rows = pl.ds(n * BLOCK, BLOCK)
-        pltpu.make_async_copy(base_s.at[rows], base_ref.at[rows], sem).start()
-        pltpu.make_async_copy(gate_s.at[rows], gate_ref.at[rows], sem).start()
+            base_s[rows] = base.astype(BF16).reshape(STEP, 128, 128)
+            gate_s[rows] = gate.astype(BF16).reshape(STEP, 128, 128)
+        if base_s is not base_ref:
+            rows = pl.ds(n * BLOCK, BLOCK)
+            pltpu.make_async_copy(base_s.at[rows], base_ref.at[rows], sem).start()
+            pltpu.make_async_copy(gate_s.at[rows], gate_ref.at[rows], sem).start()
         return carry
 
     lax.fori_loop(0, count // BLOCK, step, 0)
-    pltpu.make_async_copy(base_s, base_ref, sem).wait()
-    pltpu.make_async_copy(gate_s, gate_ref, sem).wait()
-
-
-def transition(pair, w_in, w_out, w_gate, first, count):
+    if base_s is not base_ref:
+        pltpu.make_async_copy(base_s, base_ref, sem).wait()
+        pltpu.make_async_copy(gate_s, gate_ref, sem).wait()
+
+
+def transition(pair, w_in, w_out, w_gate, first, count, keep=False):
     shape = (count,) + pair.shape[1:]
     return pl.pallas_call(
         functools.partial(transition_kernel, first),
         in_specs=[hbm()] + [vmem()] * 3,
-        out_specs=[hbm()] * 2,
-        out_shape=[pltpu.HBM(shape, BF16)] * 2,
-        scratch_shapes=[pltpu.VMEM(shape, BF16)] * 3
+        out_specs=[vmem() if keep else hbm()] * 2,
+        out_shape=[(pltpu.VMEM if keep else pltpu.HBM)(shape, BF16)] * 2,
+        scratch_shapes=[pltpu.VMEM(shape, BF16)] * (1 if keep else 3)
         + [pltpu.SemaphoreType.DMA((count // BLOCK,)), pltpu.SemaphoreType.DMA],
         compiler_params=pltpu.CompilerParams(vmem_limit_bytes=VMEM_LIMIT),
         cost_estimate=pl.CostEstimate(
@@ -392,6 +417,8 @@
         while at >= counts[part]:
             at -= counts[part]
             part += 1
+        if part == len(counts) - 1:
+            return []
         source = pl.ds(at, BLOCK)
         return [
             pltpu.make_async_copy(held[2 * part].at[source], base_s.at[rows], sems.at[n]),
@@ -451,9 +478,7 @@
             basis.append(jnp.exp(-(t * t)))
         return basis + [tail]
 
-    per = 16
-
-    def terms(start):
+    def terms(start, per):
         feats = []
         for u in range(per // 2):
             row = start + 2 * u
@@ -465,19 +490,18 @@
             term[128 * (u // 2) : 128 * (u // 2 + 1), 128 * (u % 2) : 128 * (u % 2 + 1)] for u in range(per)
         ]
 
-    def finish_held(start):
-        for u, term in enumerate(terms(start)):
-            gate = gate_s[start + u].astype(F32)
-            made_s[start + u] = (base_s[start + u].astype(F32) + gate * term).astype(BF16)
+    def finish_held(start, base_ref=base_s, gate_ref=gate_s, first=0):
+        for u, term in enumerate(terms(start, HELD_STEP)):
+            gate = gate_ref[start - first + u].astype(F32)
+            made_s[start + u] = (base_ref[start - first + u].astype(F32) + gate * term).astype(BF16)
 
     def finish_whole(start):
-        term = terms(start)
-        for i in range(0, per, 8):
-            x = base_s[pl.ds(start + i, 8)].reshape(8 * 128, 128)
-            base, gate = transition_step(x, w_up_ref[...], w_down_ref[...], half_gate)
-            for u in range(8):
-                spot = slice(128 * u, 128 * (u + 1))
-                made_s[start + i + u] = (base[spot] + gate[spot] * term[i + u]).astype(BF16)
+        term = terms(start, STEP)
+        x = base_s[pl.ds(start, STEP)].reshape(STEP * 128, 128)
+        base, gate = transition_step(x, w_up_ref[...], w_down_ref[...], half_gate)
+        for u in range(STEP):
+            spot = slice(128 * u, 128 * (u + 1))
+            made_s[start + u] = (base[spot] + gate[spot] * term[u]).astype(BF16)
 
     def send(n):
         rows = pl.ds(n * BLOCK, BLOCK)
@@ -489,15 +513,22 @@
         if pair_too:
             pltpu.make_async_copy(pair_ref.at[rows], gate_s.at[rows], sems.at[blocks + n]).wait()
 
-    def step(finish, pair_too, n, carry):
-        await_block(n, pair_too)
+    def step(finish, copies, per, n, carry):
+        if copies:
+            await_block(n, copies == 2)
         for i in range(0, BLOCK, per):
             finish(n * BLOCK + i)
         send(n)
         return carry
 
-    lax.fori_loop(0, done // BLOCK, functools.partial(step, finish_held, True), 0)
-    lax.fori_loop(done // BLOCK, blocks, functools.partial(step, finish_whole, False), 0)
+    copied = done - counts[-1]
+    finish_kept = functools.partial(
+        finish_held, base_ref=held[-2], gate_ref=held[-1], first=copied
+    )
+    kept_step = functools.partial(step, finish_kept, 0, HELD_STEP)
+    lax.fori_loop(copied // BLOCK, done // BLOCK, kept_step, 0)
+    lax.fori_loop(0, copied // BLOCK, functools.partial(step, finish_held, 2, HELD_STEP), 0)
+    lax.fori_loop(done // BLOCK, blocks, functools.partial(step, finish_whole, 1, STEP), 0)
     pltpu.make_async_copy(made_s, out_ref, sem).wait()
 
 
@@ -507,7 +538,7 @@
     blocks = pair.shape[0] // BLOCK
     return pl.pallas_call(
         functools.partial(structure_kernel, counts),
-        in_specs=[smem, smem] + [vmem()] * 7 + [hbm()] * (1 + len(held)),
+        in_specs=[smem, smem] + [vmem()] * 7 + [hbm()] * (len(held) - 1) + [vmem()] * 2,
         out_specs=hbm(),
         scratch_shapes=[pltpu.VMEM(pair.shape, BF16)] * 3
         + [
@@ -519,7 +550,7 @@
         out_shape=jax.ShapeDtypeStruct(pair.shape, BF16),
         compiler_params=pltpu.CompilerParams(vmem_limit_bytes=VMEM_LIMIT),
         name="structure",
-    )(rows, chain, cols, chain.reshape(-1, 128), w_in, w_out, w_up, w_down, w_gate, in_hbm(pair), *map(in_hbm, held))
+    )(rows, chain, cols, chain.reshape(-1, 128), w_in, w_out, w_up, w_down, w_gate, in_hbm(pair), *map(in_hbm, held[:-2]), *held[-2:])
 
 
 def exchange(v, axis):
@@ -550,25 +581,27 @@
     step = functools.partial(transition, w_in=w_trans_in, w_out=w_trans_out, w_gate=w_gate)
 
     table = exchange(records(node_state, coords, row_devices * col_devices), BOTH)
-    found, mark = select_edges(neighbours.T, pair)
+    edge, pick_col, pick_row = select_edges(neighbours.T, pair, w_edge.T)
+    pair, edge = lax.optimization_barrier((pair, edge))
+    held = step(pair, first=0, count=PARTS[0]) if PARTS[0] else []
     parts = edge_sums(
-        found,
-        mark,
+        edge,
+        pick_col,
+        pick_row,
         table.reshape(-1, 128),
-        w_edge.T,
         w_radial,
         w_query,
         w_keyval,
         w_edge_kv,
         w_move.T,
     )
-    pair, parts = lax.optimization_barrier((pair, parts))
+    pair, parts, held = lax.optimization_barrier((pair, parts, held))
     parts = exchange(parts, "col")
-    held = step(pair, first=0, count=FIRST)
+    held += step(pair, first=PARTS[0], count=PARTS[1])
     node_out, own, rows, send = totals(parts, node_state, w_out, row_devices)
-    pair, send = lax.optimization_barrier((pair, send))
+    pair, send, held = lax.optimization_barrier((pair, send, held))
     cols = exchange(send, "row")
-    held += step(pair, first=FIRST, count=SECOND)
+    held += step(pair, first=PARTS[0] + PARTS[1], count=PARTS[2], keep=True)
     pair_out = structure(
         rows, chain, cols, w_feat_in, w_feat_out, w_trans_in, w_trans_out, w_gate, pair, held
     )

time: 79 us -> 77.3 us (0.978)
  Pallas kernels: 51.6 us -> 50.2 us
    pallas_call x2, Pallas kernels: 16.7 us -> 13.1 us  [transition(): pl.pallas_call(functools.partial(transition_kernel, first), in_specs=[hbm...]
    pallas_call x1, Pallas kernels: 17.9 us -> 19.8 us  [structure(): pl.pallas_call(functools.partial(structure_kernel, counts), in_specs=[sme...]
  transfers between devices with their start and end apart: 3 -> 3, of which waited for: 1 -> 2; matrix products, arithmetic and copies ran while one was open for 0% -> 0% of each run, Pallas kernels for 30% -> 28%
where the time goes in v3:
time: 77.3 us; the launch traced here: 76.8 us
  Pallas kernels  50.2 us (65%)
  starting transfers between devices  19.6 us (25%)
  waiting for transfers between devices  5.91 us (8%)
  between operations  1.01 us (1%)
    pallas_call x1, Pallas kernels, structure(): pl.pallas_call(functools.partial(structure_kernel, counts), in_specs=[sme...  19.8 us
    all_to_all x3, starting transfers between devices, exchange(): return lax.all_to_all(v, axis, split_axis=0, concat_axis=0, tiled=True)  19.6 us
    pallas_call x2, Pallas kernels, transition(): pl.pallas_call(functools.partial(transition_kernel, first), in_specs=[hbm...  13.1 us
    pallas_call x1, Pallas kernels, select_edges(): pl.pallas_call(select_kernel, in_specs=[hbm(), hbm(), hbm()], out_specs=[...  8.68 us
    pallas_call x1, Pallas kernels, edge_sums(): pl.pallas_call(edge_kernel, grid=(1,), in_specs=[vmem()] * 4 + [whole(a.s...  6.25 us
    all_to_all x3, waiting for transfers between devices, exchange(): return lax.all_to_all(v, axis, split_axis=0, concat_axis=0, tiled=True)  5.91 us
    pallas_call x1, Pallas kernels, records(): pl.pallas_call(record_kernel, out_shape=jax.ShapeDtypeStruct((copies, GRO...  1.72 us
  transfers between devices with their start and end apart: 3, of which 2 were waited for; matrix products, arithmetic and copies ran while one was open for 0% of the time, Pallas kernels for 28%

profile of v3, /device:TPU:1, one launch (start us, length us, event | category | flops | bytes accessed | tf_op | source)
XLA Modules:
  0.0 76.8 jit_solution(18290370707954778886)
XLA Ops:
  0.6 0.0 copy-start.12
  0.6 0.0 copy-start.10
  0.7 0.0 copy-start.9
  0.7 0.0 copy-start.8
  0.7 0.0 copy-start.11
  0.7 1.7 %records.1 = bf16[128,16,128]{2,1,0:T(8,128)(2,1)} custom-call(bf16[16,64]{1,0:T(8,128)(2,1)} %node_ref.3, f32[3,3,16]{2,1,0:T(4,128)} %coords_ref.1), custom_call_target="tpu_custom_call" | custom-call | tf_op jit(solution)/shard_map/records/pallas_call | solution.py:76
  2.4 11.5 %all-to-all-start = ((bf16[128,16,128]{2,1,0:T(8,128)(2,1)}), bf16[128,16,128]{2,1,0:T(8,128)(2,1)S(1)}, u32[]{:S(2)}, u32[]{:S(2)}) async-start(bf16[128,16,128]{2,1,0:T(8,128)(2,1)} %records.1), calls=%async_computation | async-start | bytes 1048576 | tf_op jit(solution)/shard_map/all_to_all | solution.py:557
  13.9 0.0 copy-start
  13.9 0.0 copy-start.1
  13.9 0.0 copy-start.2
  13.9 8.7 %select_edges.1 = (f32[2048,128]{1,0:T(8,128)S(1)}, bf16[2048,128]{1,0:T(8,128)(2,1)S(1)}, bf16[2048,128]{1,0:T(8,128)(2,1)S(1)}) custom-call(s32[64,256]{1,0:T(8,128)} %bitcast.8, bf16[256,128,128]{2,1,0:T(8,128)(2,1)} %pair_ref.4, bf16[64,128]{1,0:T(8,128)(2,1)} %bitcast.9), custom_call_target="tpu_custom_call" | custom-call | flops 3000000000 | bytes 9437184 | tf_op jit(solution)/shard_map/select_edges/pallas_call | solution.py:174
  22.6 0.0 copy-start.5
  22.6 0.0 copy-start.6
  22.7 4.6 %all-to-all-done = bf16[128,16,128]{2,1,0:T(8,128)(2,1)S(1)} async-done(((bf16[128,16,128]{2,1,0:T(8,128)(2,1)}), bf16[128,16,128]{2,1,0:T(8,128)(2,1)S(1)}, u32[]{:S(2)}, u32[]{:S(2)}) %all-to-all-start) | async-done | bytes 524320 | tf_op jit(solution)/shard_map/all_to_all | solution.py:557
  27.2 0.0 copy-done.12
  27.2 0.0 copy-done.10
  27.3 0.0 copy-done.9
  27.3 0.0 copy-done.8
  27.3 0.0 copy-done.11
  27.3 6.2 %edge_sums.1 = f32[16,40,128]{2,1,0:T(8,128)} custom-call(f32[2048,128]{1,0:T(8,128)S(1)} %get-tuple-element.24.edge_ref, bf16[2048,128]{1,0:T(8,128)(2,1)S(1)} %get-tuple-element.25.pick_col_ref, bf16[2048,128]{1,0:T(8,128)(2,1)S(1)} %get-tuple-element.26.pick_row_ref, bf16[2048,128]{1,0:T(8,128)(2,1)S(1)} %bitcast.5, bf16[36,64]{1,0:T(8,128)(2,1)S(1)} %copy-done.11, ...), custom_call_target="tpu_custom_call" | custom-call | flops 2000000000 | bytes 3145728 | tf_op jit(solution)/shard_map/edge_sums/pallas_call | solution.py:288
  33.5 3.5 %all-to-all-start.1 = ((f32[16,40,128]{2,1,0:T(8,128)}), f32[16,40,128]{2,1,0:T(8,128)S(1)}, u32[]{:S(2)}, u32[]{:S(2)}) async-start(f32[16,40,128]{2,1,0:T(8,128)} %edge_sums.1), calls=%async_computation.1 | async-start | bytes 655360 | tf_op jit(solution)/shard_map/all_to_all | solution.py:557
  37.1 0.0 copy-done
  37.1 0.0 copy-done.1
  37.1 0.0 copy-done.2
  37.1 0.0 copy-start.3
  37.1 0.0 copy-start.4
  37.1 0.0 copy-start.7
  37.1 9.5 %transition.2 = (bf16[96,128,128]{2,1,0:T(8,128)(2,1)}, bf16[96,128,128]{2,1,0:T(8,128)(2,1)}) custom-call(bf16[256,128,128]{2,1,0:T(8,128)(2,1)} %pair_ref.4, bf16[128,256]{1,0:T(8,128)(2,1)S(1)} %copy-done, bf16[256,128]{1,0:T(8,128)(2,1)S(1)} %copy-done.1, bf16[128,128]{1,0:T(8,128)(2,1)S(1)} %copy-done.2), custom_call_target="tpu_custom_call" | custom-call | flops 2013265920 | bytes 9437184 | tf_op jit(solution)/shard_map/transition/pallas_call | solution.py:387
  46.7 0.0 all-to-all-done.1.parts_ref
  46.7 0.0 copy-done.5
  46.7 0.0 copy-done.6
  46.7 0.7 totals.1
  47.4 4.6 %all-to-all-start.2 = ((f32[8,16,128]{2,1,0:T(8,128)}), f32[8,16,128]{2,1,0:T(8,128)S(1)}, u32[]{:S(2)}, u32[]{:S(2)}) async-start(f32[8,16,128]{2,1,0:T(8,128)} %get-tuple-element.33), calls=%async_computation.2 | async-start | bytes 131072 | tf_op jit(solution)/shard_map/all_to_all | solution.py:557
  52.0 3.5 %transition.3 = (bf16[32,128,128]{2,1,0:T(8,128)(2,1)S(1)}, bf16[32,128,128]{2,1,0:T(8,128)(2,1)S(1)}) custom-call(bf16[256,128,128]{2,1,0:T(8,128)(2,1)} %pair_ref.4, bf16[128,256]{1,0:T(8,128)(2,1)S(1)} %copy-done, bf16[256,128]{1,0:T(8,128)(2,1)S(1)} %copy-done.1, bf16[128,128]{1,0:T(8,128)(2,1)S(1)} %copy-done.2), custom_call_target="tpu_custom_call" | custom-call | flops 671088640 | bytes 3145728 | tf_op jit(solution)/shard_map/transition/pallas_call | solution.py:387
  55.6 1.3 %all-to-all-done.2.cols_ref = f32[8,16,128]{2,1,0:T(8,128)S(1)} async-done(((f32[8,16,128]{2,1,0:T(8,128)}), f32[8,16,128]{2,1,0:T(8,128)S(1)}, u32[]{:S(2)}, u32[]{:S(2)}) %all-to-all-start.2) | async-done | bytes 65568 | tf_op jit(solution)/shard_map/all_to_all | solution.py:557
  56.9 0.0 copy-done.3
  56.9 0.0 copy-done.4
  56.9 0.0 copy-done.7
  56.9 19.8 %structure.1 = bf16[256,128,128]{2,1,0:T(8,128)(2,1)} custom-call(f32[16,256]{1,0:T(8,128)S(1)} %get-tuple-element.28.rows_ref, s32[2048]{0:T(1024)S(1)} %copy-done.3, f32[8,16,128]{2,1,0:T(8,128)S(1)} %all-to-all-done.2.cols_ref, s32[16,128]{1,0:T(8,128)S(1)} %bitcast.6, bf16[42,128]{1,0:T(8,128)(2,1)S(1)} %copy-done.7, bf16[128,128]{1,0:T(8,128)(2,1)S(1)} %copy-done.4, ...), custom_call_target="tpu_custom_call" | custom-call | tf_op jit(solution)/shard_map/structure/pallas_call | solution.py:539
Async XLA Ops:
  0.6 26.6 %copy-start.12 = (bf16[64,12]{0,1:T(8,128)(2,1)S(1)}, bf16[64,12]{0,1:T(8,128)(2,1)}, u32[]{:S(2)}) copy-start(bf16[64,12]{0,1:T(8,128)(2,1)} %param.28) | copy-start | bytes 4612
  0.6 26.6 %copy-start.10 = (bf16[64,128]{1,0:T(8,128)(2,1)S(1)}, bf16[64,128]{1,0:T(8,128)(2,1)}, u32[]{:S(2)}) copy-start(bf16[64,128]{1,0:T(8,128)(2,1)} %w_edge_kv_ref.1) | copy-start | bytes 49156
  0.7 26.6 %copy-start.9 = (bf16[64,128]{1,0:T(8,128)(2,1)S(1)}, bf16[64,128]{1,0:T(8,128)(2,1)}, u32[]{:S(2)}) copy-start(bf16[64,128]{1,0:T(8,128)(2,1)} %w_keyval_ref.1) | copy-start | bytes 49156
  0.7 26.6 %copy-start.8 = (bf16[64,64]{1,0:T(8,128)(2,1)S(1)}, bf16[64,64]{1,0:T(8,128)(2,1)}, u32[]{:S(2)}) copy-start(bf16[64,64]{1,0:T(8,128)(2,1)} %w_query_ref.1) | copy-start | bytes 24580
  0.7 26.6 %copy-start.11 = (bf16[36,64]{1,0:T(8,128)(2,1)S(1)}, bf16[36,64]{1,0:T(8,128)(2,1)}, u32[]{:S(2)}) copy-start(bf16[36,64]{1,0:T(8,128)(2,1)} %w_radial_ref.1) | copy-start | bytes 13828
  2.4 24.8 %all-to-all-start = ((bf16[128,16,128]{2,1,0:T(8,128)(2,1)}), bf16[128,16,128]{2,1,0:T(8,128)(2,1)S(1)}, u32[]{:S(2)}, u32[]{:S(2)}) async-start(bf16[128,16,128]{2,1,0:T(8,128)(2,1)} %records.1), calls=%async_computation | async-start | bytes 1048576 | tf_op jit(solution)/shard_map/all_to_all | solution.py:557
  13.9 23.2 %copy-start = (bf16[128,256]{1,0:T(8,128)(2,1)S(1)}, bf16[128,256]{1,0:T(8,128)(2,1)}, u32[]{:S(2)}) copy-start(bf16[128,256]{1,0:T(8,128)(2,1)} %w_up_ref.1) | copy-start | bytes 196612
  13.9 23.2 %copy-start.1 = (bf16[256,128]{1,0:T(8,128)(2,1)S(1)}, bf16[256,128]{1,0:T(8,128)(2,1)}, u32[]{:S(2)}) copy-start(bf16[256,128]{1,0:T(8,128)(2,1)} %w_down_ref.1) | copy-start | bytes 196612
  13.9 23.2 %copy-start.2 = (bf16[128,128]{1,0:T(8,128)(2,1)S(1)}, bf16[128,128]{1,0:T(8,128)(2,1)}, u32[]{:S(2)}) copy-start(bf16[128,128]{1,0:T(8,128)(2,1)} %w_gate_ref.5) | copy-start | bytes 98308
  22.6 24.0 %copy-start.5 = (bf16[16,64]{1,0:T(8,128)(2,1)S(1)}, bf16[16,64]{1,0:T(8,128)(2,1)}, u32[]{:S(2)}) copy-start(bf16[16,64]{1,0:T(8,128)(2,1)} %node_ref.3) | copy-start | bytes 6148
  22.6 24.0 %copy-start.6 = (bf16[64,64]{1,0:T(8,128)(2,1)S(1)}, bf16[64,64]{1,0:T(8,128)(2,1)}, u32[]{:S(2)}) copy-start(bf16[64,64]{1,0:T(8,128)(2,1)} %w_out_ref.4) | copy-start | bytes 24580
  33.5 13.1 %all-to-all-start.1 = ((f32[16,40,128]{2,1,0:T(8,128)}), f32[16,40,128]{2,1,0:T(8,128)S(1)}, u32[]{:S(2)}, u32[]{:S(2)}) async-start(f32[16,40,128]{2,1,0:T(8,128)} %edge_sums.1), calls=%async_computation.1 | async-start | bytes 655360 | tf_op jit(solution)/shard_map/all_to_all | solution.py:557
  37.1 19.8 %copy-start.3 = (s32[2048]{0:T(1024)S(1)}, s32[2048]{0:T(1024)}, u32[]{:S(2)}) copy-start(s32[2048]{0:T(1024)} %chain_ref.1) | copy-start | bytes 24580
  37.1 19.8 %copy-start.4 = (bf16[128,128]{1,0:T(8,128)(2,1)S(1)}, bf16[128,128]{1,0:T(8,128)(2,1)}, u32[]{:S(2)}) copy-start(bf16[128,128]{1,0:T(8,128)(2,1)} %w_out_ref.7) | copy-start | bytes 98308
  37.1 19.8 %copy-start.7 = (bf16[42,128]{1,0:T(8,128)(2,1)S(1)}, bf16[42,128]{1,0:T(8,128)(2,1)}, u32[]{:S(2)}) copy-start(bf16[42,128]{1,0:T(8,128)(2,1)} %w_in_ref.5) | copy-start | bytes 32260
  47.4 9.5 %all-to-all-start.2 = ((f32[8,16,128]{2,1,0:T(8,128)}), f32[8,16,128]{2,1,0:T(8,128)S(1)}, u32[]{:S(2)}, u32[]{:S(2)}) async-start(f32[8,16,128]{2,1,0:T(8,128)} %get-tuple-element.33), calls=%async_computation.2 | async-start | bytes 131072 | tf_op jit(solution)/shard_map/all_to_all | solution.py:557

commit v4 on v3

--- a/solution.py
+++ b/solution.py
@@ -214,16 +214,19 @@
     for ref in (w_keyval_s, w_query_s, w_radial_s, w_mix_s, w_move_s):
         ref[...] = jnp.zeros_like(ref)
     w_keyval_s[0:64, :] = w_keyval_ref[...]
-    w_query_s[0:64, 0:64] = w_query_ref[...]
-    w_radial_s[0:36, 0:64] = w_radial_ref[...]
-    w_mix_s[0:64, :] = w_edge_kv_ref[...]
-    w_move_s[0:12, 0:64] = w_move_ref[...]
+    w_query_s[0:64, 0:64] = (-w_query_ref[...].astype(F32)).astype(BF16)
+    w_radial_s[0:36, 0:64] = w_radial_ref[...].astype(F32)
+    w_radial = w_radial_s[...].astype(BF16)
+    w_mix_s[0:64, 0:128] = w_edge_kv_ref[...]
+    w_move_s[0:12, 0:64] = w_move_ref[...].astype(F32)
+    w_mix_s[:, 128:256] = jnp.transpose(w_move_s[...]).astype(BF16)
     rows = table_ref[pl.ds(pl.multiple_of(lax.axis_index("row") * 256, 256), 256), :]
     rows_ref[...] = rows
     cols = table_ref[pl.ds(pl.multiple_of(col * 128, 128), 128), :]
     keyval = dot(cols, w_keyval_s[...]).astype(BF16)
+    lane = iota((1, 128), 1)
+    cols = jnp.where(lane < PIECES, 0.0, cols.astype(F32)).astype(BF16)
     by_column = jnp.concatenate([keyval, cols], axis=1)
-    lane = iota((1, 128), 1)
     source = iota((256, 256), 0)
     target = iota((256, 256), 1)
     channel = jnp.bitwise_and(source, 127)
@@ -248,19 +251,22 @@
         pick_col = pick_col_ref[spots, :]
         pick_row = pick_row_ref[spots, :]
         rows = rows_ref[pl.ds(step * own, own), :]
-        from_col = dot(pick_col, by_column)
-        from_row = dot(pick_row, rows)
-        gap = from_col[:, 128:] - from_row
+        by_row = jnp.concatenate([jnp.zeros_like(rows), (-rows.astype(F32)).astype(BF16)], axis=1)
+        picked = dot(
+            jnp.concatenate([pick_col, pick_row], axis=1), jnp.concatenate([by_column, by_row], axis=0)
+        )
+        gap = picked[:, 128:]
         relative = gap + pltpu.roll(gap, 112, 1) + pltpu.roll(gap, 96, 1)
         distance = jnp.sqrt(jnp.sum(relative * relative * alpha, axis=1, keepdims=True))
         offset = (distance - centre) * 2.0
         basis = jnp.exp(-(offset * offset)).astype(BF16)
-        hidden = silu(edge_ref[spots, :] + dot(basis, w_radial_s[...])).astype(BF16)
-        keyval_edge = from_col[:, :128] + dot(hidden, w_mix_s[...])
-        queries = dot(from_row.astype(BF16), w_query_s[...])
+        hidden = silu(edge_ref[spots, :] + dot(basis, w_radial)).astype(BF16)
+        mix = dot(hidden, w_mix_s[...])
+        keyval_edge = picked[:, :128] + mix[:, :128]
+        queries = dot(gap.astype(BF16), w_query_s[...])
         attention = 0.5 * jnp.tanh(dot(split2(queries * keyval_edge), heads)) + 0.5
         values = attention[:, :128] * keyval_edge
-        moves = attention[:, 128:] * dot_nt(hidden, w_move_s[...])
+        moves = attention[:, 128:] * mix[:, 128:]
         move = dot(split2(moves), spread) * relative
         both = jnp.where(lane < 64, pltpu.roll(move, 64, 1), values)
         summed = dot_t(pick_row, split2(both))
@@ -290,7 +296,13 @@
         grid=(1,),
         in_specs=[vmem()] * 4 + [whole(a.shape) for a in operands[4:]],
         out_specs=whole((groups, 40, 128)),
-        scratch_shapes=[pltpu.VMEM((128, 128), BF16)] * 5 + [pltpu.VMEM((groups * GROUP, 128), BF16)],
+        scratch_shapes=[pltpu.VMEM((128, 128), BF16)] * 2
+        + [
+            pltpu.VMEM((128, 128), F32),
+            pltpu.VMEM((128, 256), BF16),
+            pltpu.VMEM((128, 128), F32),
+            pltpu.VMEM((groups * GROUP, 128), BF16),
+        ],
         out_shape=jax.ShapeDtypeStruct((groups, 40, 128), F32),
         compiler_params=pltpu.CompilerParams(vmem_limit_bytes=VMEM_LIMIT),
         cost_estimate=pl.CostEstimate(flops=2_000_000_000, bytes_accessed=3 * 2**20, transcendentals=0),
@@ -403,7 +415,7 @@
     counts, rows_ref, chain_ref, cols_ref, chains_ref, w_in_ref, w_out_ref, w_up_ref, w_down_ref, w_gate_ref, pair_ref, *refs
 ):
     held = refs[: 2 * len(counts)]
-    out_ref, base_s, gate_s, made_s, w_in_s, w_out_s, sems, sem = refs[2 * len(counts) :]
+    out_ref, base_s, gate_s, made_s, w_in_f, w_in_s, w_out_s, sems, sem = refs[2 * len(counts) :]
     done = sum(counts)
     total = base_s.shape[0]
     blocks = total // BLOCK
@@ -430,13 +442,14 @@
             copy.start()
     row_index = lax.axis_index("row")
     col_index = lax.axis_index("col")
-    w_in_s[...] = jnp.zeros_like(w_in_s)
+    w_in_f[...] = jnp.zeros_like(w_in_f)
     w_out_s[...] = jnp.zeros_like(w_out_s)
-    half = halved(w_in_ref)
+    half = w_in_ref[...].astype(F32) * 0.5
     for k in range(2):
-        w_in_s[48 * k : 48 * k + 36, 128 * k : 128 * (k + 1)] = half[0:36]
-        w_in_s[48 * k + 40 : 48 * k + 46, 128 * k : 128 * (k + 1)] = half[36:42]
+        w_in_f[48 * k : 48 * k + 36, 128 * k : 128 * (k + 1)] = half[0:36]
+        w_in_f[48 * k + 40 : 48 * k + 46, 128 * k : 128 * (k + 1)] = half[36:42]
         w_out_s[128 * k : 128 * (k + 1), 128 * k : 128 * (k + 1)] = halved(w_out_ref)
+    w_in_s[...] = w_in_f[...].astype(BF16)
     half_gate = halved(w_gate_ref)
 
     cols = cols_ref[lax.shift_right_logical(col_index, 1)]
@@ -542,6 +555,7 @@
         out_specs=hbm(),
         scratch_shapes=[pltpu.VMEM(pair.shape, BF16)] * 3
         + [
+            pltpu.VMEM((96, 256), F32),
             pltpu.VMEM((96, 256), BF16),
             pltpu.VMEM((256, 256), BF16),
             pltpu.SemaphoreType.DMA((2 * blocks,)),

time: 77.3 us -> 77.3 us (level)
  no operation moved by 1% of the time
where the time goes in v4:
time: 77.3 us; the launch traced here: 76.8 us
  Pallas kernels  50.2 us (65%)
  starting transfers between devices  19.6 us (25%)
  waiting for transfers between devices  5.91 us (8%)
  between operations  1.01 us (1%)
    pallas_call x1, Pallas kernels, structure(): pl.pallas_call(functools.partial(structure_kernel, counts), in_specs=[sme...  19.8 us
    all_to_all x3, starting transfers between devices, exchange(): return lax.all_to_all(v, axis, split_axis=0, concat_axis=0, tiled=True)  19.6 us
    pallas_call x2, Pallas kernels, transition(): pl.pallas_call(functools.partial(transition_kernel, first), in_specs=[hbm...  13 us
    pallas_call x1, Pallas kernels, select_edges(): pl.pallas_call(select_kernel, in_specs=[hbm(), hbm(), hbm()], out_specs=[...  8.68 us
    pallas_call x1, Pallas kernels, edge_sums(): pl.pallas_call(edge_kernel, grid=(1,), in_specs=[vmem()] * 4 + [whole(a.s...  6.21 us
    all_to_all x3, waiting for transfers between devices, exchange(): return lax.all_to_all(v, axis, split_axis=0, concat_axis=0, tiled=True)  5.91 us
    pallas_call x1, Pallas kernels, records(): pl.pallas_call(record_kernel, out_shape=jax.ShapeDtypeStruct((copies, GRO...  1.72 us
  transfers between devices with their start and end apart: 3, of which 2 were waited for; matrix products, arithmetic and copies ran while one was open for 0% of the time, Pallas kernels for 28%

profile of v4, /device:TPU:1, one launch (start us, length us, event | category | flops | bytes accessed | tf_op | source)
XLA Modules:
  0.0 76.8 jit_solution(867011401168089304)
XLA Ops:
  0.6 0.0 copy-start.12
  0.6 0.0 copy-start.10
  0.7 0.0 copy-start.9
  0.7 0.0 copy-start.8
  0.7 0.0 copy-start.11
  0.7 1.7 %records.1 = bf16[128,16,128]{2,1,0:T(8,128)(2,1)} custom-call(bf16[16,64]{1,0:T(8,128)(2,1)} %node_ref.3, f32[3,3,16]{2,1,0:T(4,128)} %coords_ref.1), custom_call_target="tpu_custom_call" | custom-call | tf_op jit(solution)/shard_map/records/pallas_call | solution.py:76
  2.4 11.5 %all-to-all-start = ((bf16[128,16,128]{2,1,0:T(8,128)(2,1)}), bf16[128,16,128]{2,1,0:T(8,128)(2,1)S(1)}, u32[]{:S(2)}, u32[]{:S(2)}) async-start(bf16[128,16,128]{2,1,0:T(8,128)(2,1)} %records.1), calls=%async_computation | async-start | bytes 1048576 | tf_op jit(solution)/shard_map/all_to_all | solution.py:571
  13.9 0.0 copy-start
  13.9 0.0 copy-start.1
  13.9 0.0 copy-start.2
  13.9 8.7 %select_edges.1 = (f32[2048,128]{1,0:T(8,128)S(1)}, bf16[2048,128]{1,0:T(8,128)(2,1)S(1)}, bf16[2048,128]{1,0:T(8,128)(2,1)S(1)}) custom-call(s32[64,256]{1,0:T(8,128)} %bitcast.8, bf16[256,128,128]{2,1,0:T(8,128)(2,1)} %pair_ref.4, bf16[64,128]{1,0:T(8,128)(2,1)} %bitcast.9), custom_call_target="tpu_custom_call" | custom-call | flops 3000000000 | bytes 9437184 | tf_op jit(solution)/shard_map/select_edges/pallas_call | solution.py:174
  22.6 0.0 copy-start.5
  22.6 0.0 copy-start.6
  22.7 4.6 %all-to-all-done = bf16[128,16,128]{2,1,0:T(8,128)(2,1)S(1)} async-done(((bf16[128,16,128]{2,1,0:T(8,128)(2,1)}), bf16[128,16,128]{2,1,0:T(8,128)(2,1)S(1)}, u32[]{:S(2)}, u32[]{:S(2)}) %all-to-all-start) | async-done | bytes 524320 | tf_op jit(solution)/shard_map/all_to_all | solution.py:571
  27.2 0.0 copy-done.12
  27.2 0.0 copy-done.10
  27.3 0.0 copy-done.9
  27.3 0.0 copy-done.8
  27.3 0.0 copy-done.11
  27.3 6.2 %edge_sums.1 = f32[16,40,128]{2,1,0:T(8,128)} custom-call(f32[2048,128]{1,0:T(8,128)S(1)} %get-tuple-element.24.edge_ref, bf16[2048,128]{1,0:T(8,128)(2,1)S(1)} %get-tuple-element.25.pick_col_ref, bf16[2048,128]{1,0:T(8,128)(2,1)S(1)} %get-tuple-element.26.pick_row_ref, bf16[2048,128]{1,0:T(8,128)(2,1)S(1)} %bitcast.5, bf16[36,64]{1,0:T(8,128)(2,1)S(1)} %copy-done.11, ...), custom_call_target="tpu_custom_call" | custom-call | flops 2000000000 | bytes 3145728 | tf_op jit(solution)/shard_map/edge_sums/pallas_call | solution.py:294
  33.5 3.5 %all-to-all-start.1 = ((f32[16,40,128]{2,1,0:T(8,128)}), f32[16,40,128]{2,1,0:T(8,128)S(1)}, u32[]{:S(2)}, u32[]{:S(2)}) async-start(f32[16,40,128]{2,1,0:T(8,128)} %edge_sums.1), calls=%async_computation.1 | async-start | bytes 655360 | tf_op jit(solution)/shard_map/all_to_all | solution.py:571
  37.0 0.0 copy-done
  37.1 0.0 copy-done.1
  37.1 0.0 copy-done.2
  37.1 0.0 copy-start.3
  37.1 0.0 copy-start.4
  37.1 0.0 copy-start.7
  37.1 9.5 %transition.2 = (bf16[96,128,128]{2,1,0:T(8,128)(2,1)}, bf16[96,128,128]{2,1,0:T(8,128)(2,1)}) custom-call(bf16[256,128,128]{2,1,0:T(8,128)(2,1)} %pair_ref.4, bf16[128,256]{1,0:T(8,128)(2,1)S(1)} %copy-done, bf16[256,128]{1,0:T(8,128)(2,1)S(1)} %copy-done.1, bf16[128,128]{1,0:T(8,128)(2,1)S(1)} %copy-done.2), custom_call_target="tpu_custom_call" | custom-call | flops 2013265920 | bytes 9437184 | tf_op jit(solution)/shard_map/transition/pallas_call | solution.py:399
  46.6 0.0 all-to-all-done.1.parts_ref
  46.6 0.0 copy-done.5
  46.6 0.0 copy-done.6
  46.7 0.7 totals.1
  47.4 4.6 %all-to-all-start.2 = ((f32[8,16,128]{2,1,0:T(8,128)}), f32[8,16,128]{2,1,0:T(8,128)S(1)}, u32[]{:S(2)}, u32[]{:S(2)}) async-start(f32[8,16,128]{2,1,0:T(8,128)} %get-tuple-element.33), calls=%async_computation.2 | async-start | bytes 131072 | tf_op jit(solution)/shard_map/all_to_all | solution.py:571
  52.0 3.5 %transition.3 = (bf16[32,128,128]{2,1,0:T(8,128)(2,1)S(1)}, bf16[32,128,128]{2,1,0:T(8,128)(2,1)S(1)}) custom-call(bf16[256,128,128]{2,1,0:T(8,128)(2,1)} %pair_ref.4, bf16[128,256]{1,0:T(8,128)(2,1)S(1)} %copy-done, bf16[256,128]{1,0:T(8,128)(2,1)S(1)} %copy-done.1, bf16[128,128]{1,0:T(8,128)(2,1)S(1)} %copy-done.2), custom_call_target="tpu_custom_call" | custom-call | flops 671088640 | bytes 3145728 | tf_op jit(solution)/shard_map/transition/pallas_call | solution.py:399
  55.5 1.3 %all-to-all-done.2.cols_ref = f32[8,16,128]{2,1,0:T(8,128)S(1)} async-done(((f32[8,16,128]{2,1,0:T(8,128)}), f32[8,16,128]{2,1,0:T(8,128)S(1)}, u32[]{:S(2)}, u32[]{:S(2)}) %all-to-all-start.2) | async-done | bytes 65568 | tf_op jit(solution)/shard_map/all_to_all | solution.py:571
  56.9 0.0 copy-done.3
  56.9 0.0 copy-done.4
  56.9 0.0 copy-done.7
  56.9 19.8 %structure.1 = bf16[256,128,128]{2,1,0:T(8,128)(2,1)} custom-call(f32[16,256]{1,0:T(8,128)S(1)} %get-tuple-element.28.rows_ref, s32[2048]{0:T(1024)S(1)} %copy-done.3, f32[8,16,128]{2,1,0:T(8,128)S(1)} %all-to-all-done.2.cols_ref, s32[16,128]{1,0:T(8,128)S(1)} %bitcast.6, bf16[42,128]{1,0:T(8,128)(2,1)S(1)} %copy-done.7, bf16[128,128]{1,0:T(8,128)(2,1)S(1)} %copy-done.4, ...), custom_call_target="tpu_custom_call" | custom-call | tf_op jit(solution)/shard_map/structure/pallas_call | solution.py:552
Async XLA Ops:
  0.6 26.6 %copy-start.12 = (bf16[64,12]{0,1:T(8,128)(2,1)S(1)}, bf16[64,12]{0,1:T(8,128)(2,1)}, u32[]{:S(2)}) copy-start(bf16[64,12]{0,1:T(8,128)(2,1)} %param.28) | copy-start | bytes 4612
  0.6 26.6 %copy-start.10 = (bf16[64,128]{1,0:T(8,128)(2,1)S(1)}, bf16[64,128]{1,0:T(8,128)(2,1)}, u32[]{:S(2)}) copy-start(bf16[64,128]{1,0:T(8,128)(2,1)} %w_edge_kv_ref.1) | copy-start | bytes 49156
  0.7 26.6 %copy-start.9 = (bf16[64,128]{1,0:T(8,128)(2,1)S(1)}, bf16[64,128]{1,0:T(8,128)(2,1)}, u32[]{:S(2)}) copy-start(bf16[64,128]{1,0:T(8,128)(2,1)} %w_keyval_ref.1) | copy-start | bytes 49156
  0.7 26.6 %copy-start.8 = (bf16[64,64]{1,0:T(8,128)(2,1)S(1)}, bf16[64,64]{1,0:T(8,128)(2,1)}, u32[]{:S(2)}) copy-start(bf16[64,64]{1,0:T(8,128)(2,1)} %w_query_ref.1) | copy-start | bytes 24580
  0.7 26.6 %copy-start.11 = (bf16[36,64]{1,0:T(8,128)(2,1)S(1)}, bf16[36,64]{1,0:T(8,128)(2,1)}, u32[]{:S(2)}) copy-start(bf16[36,64]{1,0:T(8,128)(2,1)} %w_radial_ref.1) | copy-start | bytes 13828
  2.4 24.8 %all-to-all-start = ((bf16[128,16,128]{2,1,0:T(8,128)(2,1)}), bf16[128,16,128]{2,1,0:T(8,128)(2,1)S(1)}, u32[]{:S(2)}, u32[]{:S(2)}) async-start(bf16[128,16,128]{2,1,0:T(8,128)(2,1)} %records.1), calls=%async_computation | async-start | bytes 1048576 | tf_op jit(solution)/shard_map/all_to_all | solution.py:571
  13.9 23.1 %copy-start = (bf16[128,256]{1,0:T(8,128)(2,1)S(1)}, bf16[128,256]{1,0:T(8,128)(2,1)}, u32[]{:S(2)}) copy-start(bf16[128,256]{1,0:T(8,128)(2,1)} %w_up_ref.1) | copy-start | bytes 196612
  13.9 23.1 %copy-start.1 = (bf16[256,128]{1,0:T(8,128)(2,1)S(1)}, bf16[256,128]{1,0:T(8,128)(2,1)}, u32[]{:S(2)}) copy-start(bf16[256,128]{1,0:T(8,128)(2,1)} %w_down_ref.1) | copy-start | bytes 196612
  13.9 23.1 %copy-start.2 = (bf16[128,128]{1,0:T(8,128)(2,1)S(1)}, bf16[128,128]{1,0:T(8,128)(2,1)}, u32[]{:S(2)}) copy-start(bf16[128,128]{1,0:T(8,128)(2,1)} %w_gate_ref.5) | copy-start | bytes 98308
  22.6 24.0 %copy-start.5 = (bf16[16,64]{1,0:T(8,128)(2,1)S(1)}, bf16[16,64]{1,0:T(8,128)(2,1)}, u32[]{:S(2)}) copy-start(bf16[16,64]{1,0:T(8,128)(2,1)} %node_ref.3) | copy-start | bytes 6148
  22.6 24.0 %copy-start.6 = (bf16[64,64]{1,0:T(8,128)(2,1)S(1)}, bf16[64,64]{1,0:T(8,128)(2,1)}, u32[]{:S(2)}) copy-start(bf16[64,64]{1,0:T(8,128)(2,1)} %w_out_ref.4) | copy-start | bytes 24580
  33.5 13.1 %all-to-all-start.1 = ((f32[16,40,128]{2,1,0:T(8,128)}), f32[16,40,128]{2,1,0:T(8,128)S(1)}, u32[]{:S(2)}, u32[]{:S(2)}) async-start(f32[16,40,128]{2,1,0:T(8,128)} %edge_sums.1), calls=%async_computation.1 | async-start | bytes 655360 | tf_op jit(solution)/shard_map/all_to_all | solution.py:571
  37.1 19.8 %copy-start.3 = (s32[2048]{0:T(1024)S(1)}, s32[2048]{0:T(1024)}, u32[]{:S(2)}) copy-start(s32[2048]{0:T(1024)} %chain_ref.1) | copy-start | bytes 24580
  37.1 19.8 %copy-start.4 = (bf16[128,128]{1,0:T(8,128)(2,1)S(1)}, bf16[128,128]{1,0:T(8,128)(2,1)}, u32[]{:S(2)}) copy-start(bf16[128,128]{1,0:T(8,128)(2,1)} %w_out_ref.7) | copy-start | bytes 98308
  37.1 19.8 %copy-start.7 = (bf16[42,128]{1,0:T(8,128)(2,1)S(1)}, bf16[42,128]{1,0:T(8,128)(2,1)}, u32[]{:S(2)}) copy-start(bf16[42,128]{1,0:T(8,128)(2,1)} %w_in_ref.5) | copy-start | bytes 32260
  47.4 9.5 %all-to-all-start.2 = ((f32[8,16,128]{2,1,0:T(8,128)}), f32[8,16,128]{2,1,0:T(8,128)S(1)}, u32[]{:S(2)}, u32[]{:S(2)}) async-start(f32[8,16,128]{2,1,0:T(8,128)} %get-tuple-element.33), calls=%async_computation.2 | async-start | bytes 131072 | tf_op jit(solution)/shard_map/all_to_all | solution.py:571
